TPU v7x, 32 devices: a whole 2x2x4 slice. The times are simulated.
32 devices in a mesh: dp: 4 (over z), seq: 8 (over y, x, core).
Axes of the slice: x: 2, y: 2, z: 4, core: 2. Of those that a mesh axis runs over, the one named last changes fastest.
Arguments:
- tokens: bfloat16 [4, 2, 1024, 2048], P('dp', None, 'seq'), may hold values from -6 to 6
- doc_lengths: int32 [4, 2, 8], P('dp'), may hold values from 1 to 1017, as said below
- w_query: bfloat16 [2048, 256], P('dp'), may hold values from -0.125 to 0.125
- w_key: bfloat16 [2048, 256], P('dp'), may hold values from -0.125 to 0.125
- w_value: bfloat16 [2048, 2048], P('dp'), may hold values from -0.125 to 0.125
- w_out: bfloat16 [2048, 2048], P('dp'), may hold values from -1 to 1
- w_gate: bfloat16 [2048, 5632], P('dp'), may hold values from -0.125 to 0.125
- w_up: bfloat16 [2048, 5632], P('dp'), may hold values from -0.125 to 0.125
- w_down: bfloat16 [5632, 2048], P('dp'), may hold values from -0.078125 to 0.078125
- gain_attn: bfloat16 [2048], P('dp'), may hold values from 0.5 to 1.5
- gain_mlp: bfloat16 [2048], P('dp'), may hold values from 0.5 to 1.5
- cotangent: bfloat16 [4, 2, 1024, 2048], P('dp', None, 'seq'), may hold values from -6 to 6
Outputs:
- output: bfloat16 [4, 2, 1024, 2048], P('dp', None, 'seq')
- input_grad: float32 [4, 2, 1024, 2048], P('dp', None, 'seq')
- grad_query: float32 [2048, 256], P(('dp', 'seq'))
- grad_key: float32 [2048, 256], P(('dp', 'seq'))
- grad_value: float32 [2048, 2048], P(('dp', 'seq'))
- grad_out: float32 [2048, 2048], P(('dp', 'seq'))
- grad_gate: float32 [2048, 5632], P(('dp', 'seq'))
- grad_up: float32 [2048, 5632], P(('dp', 'seq'))
- grad_down: float32 [5632, 2048], P(('dp', 'seq'))
- grad_gain_attn: float32 [2048], P(('dp', 'seq'))
- grad_gain_mlp: float32 [2048], P(('dp', 'seq'))
Inputs may be any that keep to these rules, and one draw needn't show every extreme that they name: `doc_lengths`: in every stream the 8 lengths add up to 1024; one document of each stream, at a place drawn from the seed, holds all tokens but fewer than 128 before it and fewer than 128 after it; in one stream, drawn from the seed, every other document has one token.
All inputs are finite; a program needn't handle non-finite values.
Results may differ from a plain program's by a relative error of at most 0.02.
Values may be sent and summed in bfloat16 or wider, within the bound.
A program may use at most 640 MiB of HBM per device.

v0:
```python
import functools
import math

import jax
import jax.numpy as jnp
from jax import lax
from jax.experimental import pallas as pl
from jax.experimental.pallas import tpu as pltpu
from jax.sharding import PartitionSpec as P

D = 2048
HEADS = 16
QK_DIM = 16
FF = 5632
HEAD_V = 128
epsilon = 1e-06
MIB = 1024 * 1024


def dot(left, right):
    return jnp.dot(left, right, preferred_element_type=jnp.float32)


def contract(left, right, left_dim, right_dim):
    return lax.dot_general(
        left, right, (((left_dim,), (right_dim,)), ((), ())), preferred_element_type=jnp.float32
    )


def head_lanes(rows, head):
    lane = lax.broadcasted_iota(jnp.int32, rows.shape, 1)
    inside = (lane >= head * QK_DIM) & (lane < (head + 1) * QK_DIM)
    return jnp.where(inside, rows, jnp.zeros_like(rows))


def weights_of(query, key, head, first, base):
    scores = contract(head_lanes(query, head), key, 1, 1)
    row = base + lax.broadcasted_iota(jnp.int32, scores.shape, 0)
    column = lax.broadcasted_iota(jnp.int32, scores.shape, 1)
    mask = (column <= row) & (column >= first)
    poly = 1.0 + scores * (1.0 / math.sqrt(QK_DIM)) + scores * scores * (0.5 / QK_DIM)
    return scores, mask, jnp.where(mask, poly, 0.0)


def attend_kernel(heads, q_ref, k_ref, v_ref, first_ref, out_ref):
    rows = q_ref.shape[1]
    base = pl.program_id(1) * rows
    for head in range(heads):
        columns = slice(head * HEAD_V, (head + 1) * HEAD_V)
        unused, unused_mask, weight = weights_of(
            q_ref[0], k_ref[0], head, first_ref[0], base
        )
        denom = jnp.sum(weight, axis=1, keepdims=True)
        numer = dot(weight.astype(jnp.bfloat16), v_ref[0, :, columns])
        out_ref[0, :, columns] = (numer / denom).astype(jnp.bfloat16)


def attend(query, key, value, first, heads):
    streams, length, width = query.shape
    rows = min(256, length)
    return pl.pallas_call(
        functools.partial(attend_kernel, heads),
        grid=(streams, length // rows),
        in_specs=[
            pl.BlockSpec((1, rows, width), lambda m, i: (m, i, 0)),
            pl.BlockSpec((1, length, width), lambda m, i: (m, 0, 0)),
            pl.BlockSpec((1, length, heads * HEAD_V), lambda m, i: (m, 0, 0)),
            pl.BlockSpec((1, rows, 1), lambda m, i: (m, i, 0)),
        ],
        out_specs=pl.BlockSpec((1, rows, heads * HEAD_V), lambda m, i: (m, i, 0)),
        out_shape=jax.ShapeDtypeStruct(value.shape, jnp.bfloat16),
        compiler_params=pltpu.CompilerParams(vmem_limit_bytes=48 * MIB),
        name="attend",
    )(query, key, value, first)


def attend_back_kernel(
    heads, q_ref, k_ref, v_ref, first_ref, att_ref, g_ref, gq_ref, gk_ref, gv_ref, gk_sum, gv_sum
):
    rows = q_ref.shape[1]
    step = pl.program_id(1)
    base = step * rows

    @pl.when(step == 0)
    def _():
        gk_sum[...] = jnp.zeros_like(gk_sum)
        gv_sum[...] = jnp.zeros_like(gv_sum)

    query, key = q_ref[0], k_ref[0]
    g_query = jnp.zeros(query.shape, jnp.float32)
    for head in range(heads):
        columns = slice(head * HEAD_V, (head + 1) * HEAD_V)
        scores, mask, weight = weights_of(query, key, head, first_ref[0], base)
        denom = jnp.sum(weight, axis=1, keepdims=True)
        a = (g_ref[0, :, columns].astype(jnp.float32) / denom).astype(jnp.bfloat16)
        b = -jnp.sum(
            a.astype(jnp.float32) * att_ref[0, :, columns].astype(jnp.float32),
            axis=1,
            keepdims=True,
        )
        g_weight = contract(a, v_ref[0, :, columns], 1, 1) + b
        slope = 1.0 / math.sqrt(QK_DIM) + scores * (1.0 / QK_DIM)
        g_scores = jnp.where(mask, g_weight * slope, 0.0).astype(jnp.bfloat16)
        g_query += head_lanes(dot(g_scores, key), head)
        gk_sum[...] += contract(g_scores, head_lanes(query, head), 0, 0)
        gv_sum[:, columns] += contract(weight.astype(jnp.bfloat16), a, 0, 0)
    gq_ref[0] = g_query.astype(jnp.bfloat16)

    @pl.when(step == pl.num_programs(1) - 1)
    def _():
        gk_ref[0] = gk_sum[...].astype(jnp.bfloat16)
        gv_ref[0] = gv_sum[...].astype(jnp.bfloat16)


def attend_back(query, key, value, first, attended, grad, heads):
    streams, length, width = query.shape
    rows = min(256, length)
    some = pl.BlockSpec((1, rows, width), lambda m, i: (m, i, 0))
    all_narrow = pl.BlockSpec((1, length, width), lambda m, i: (m, 0, 0))
    all_wide = pl.BlockSpec((1, length, heads * HEAD_V), lambda m, i: (m, 0, 0))
    some_wide = pl.BlockSpec((1, rows, heads * HEAD_V), lambda m, i: (m, i, 0))
    return pl.pallas_call(
        functools.partial(attend_back_kernel, heads),
        grid=(streams, length // rows),
        in_specs=[
            some,
            all_narrow,
            all_wide,
            pl.BlockSpec((1, rows, 1), lambda m, i: (m, i, 0)),
            some_wide,
            some_wide,
        ],
        out_specs=[some, all_narrow, all_wide],
        out_shape=[
            jax.ShapeDtypeStruct(query.shape, jnp.bfloat16),
            jax.ShapeDtypeStruct(key.shape, jnp.bfloat16),
            jax.ShapeDtypeStruct(value.shape, jnp.bfloat16),
        ],
        scratch_shapes=[
            pltpu.VMEM((length, width), jnp.float32),
            pltpu.VMEM((length, heads * HEAD_V), jnp.float32),
        ],
        compiler_params=pltpu.CompilerParams(vmem_limit_bytes=56 * MIB),
        name="attend_back",
    )(query, key, value, first, attended, grad)

MESH = pl.DeviceIdType.MESH
LOW = jnp.bfloat16


def partners():
    me = lax.axis_index("seq")
    core, x, y = me % 2, me // 2 % 2, me // 4
    return me, me + 1 - 2 * core, me + 2 - 4 * x, me + 4 - 8 * y


def greet(others):
    barrier = pltpu.get_barrier_semaphore()
    for other in others:
        pl.semaphore_signal(barrier, inc=1, device_id={"seq": other}, device_id_type=MESH)
    pl.semaphore_wait(barrier, len(others))


def remote(send, recv, k, src, dst, to):
    return pltpu.make_async_remote_copy(
        src_ref=src,
        dst_ref=dst,
        send_sem=send.at[k],
        recv_sem=recv.at[k],
        device_id={"seq": to},
        device_id_type=MESH,
    )


def gather_kernel(x_ref, o_ref, send, recv, own_sem):
    me, sib, xn, yn = partners()
    diag = xn + yn - me
    half = x_ref.shape[0] // 2
    copy = functools.partial(remote, send, recv)
    upper, lower = pl.ds(0, half), pl.ds(half, half)
    greet((sib, xn, yn))
    own = pltpu.make_async_copy(x_ref, o_ref.at[me], own_sem)
    own.start()
    xa = copy(0, x_ref.at[upper], o_ref.at[me, upper], xn)
    yb = copy(1, x_ref.at[lower], o_ref.at[me, lower], yn)
    xb = copy(2, x_ref.at[lower], o_ref.at[me, lower], xn)
    ya = copy(3, x_ref.at[upper], o_ref.at[me, upper], yn)
    beside = [copy(4, x_ref, o_ref.at[me], sib)]
    started = [xa, yb, xb, ya, beside[0]]
    for c in started:
        c.start()

    def pass_on(k, origin, part, to):
        block = o_ref.at[origin, part]
        c = copy(k, block, block, to)
        c.start()
        started.append(c)
        return c

    xa.wait_recv()
    fy = pass_on(5, xn, upper, yn)
    beside.append(pass_on(6, xn, upper, sib))
    yb.wait_recv()
    fx = pass_on(7, yn, lower, xn)
    beside.append(pass_on(8, yn, lower, sib))
    xb.wait_recv()
    beside.append(pass_on(9, xn, lower, sib))
    ya.wait_recv()
    beside.append(pass_on(10, yn, upper, sib))
    fy.wait_recv()
    beside.append(pass_on(11, diag, upper, sib))
    fx.wait_recv()
    beside.append(pass_on(12, diag, lower, sib))
    own.wait()
    for c in beside:
        c.wait_recv()
    for c in started:
        c.wait_send()


def moved(nbytes):
    return pl.CostEstimate(flops=0, bytes_accessed=nbytes * 10, transcendentals=0)


def gather_plane(x, number):
    pieces = lax.axis_size("seq")
    if pieces != 8:
        return lax.all_gather(x, "seq", axis=0)
    return pl.pallas_call(
        gather_kernel,
        out_shape=jax.ShapeDtypeStruct((8,) + x.shape, x.dtype),
        in_specs=[pl.BlockSpec(memory_space=pl.ANY)],
        out_specs=pl.BlockSpec(memory_space=pl.ANY),
        scratch_shapes=[
            pltpu.SemaphoreType.DMA((13,)),
            pltpu.SemaphoreType.DMA((13,)),
            pltpu.SemaphoreType.DMA,
        ],
        compiler_params=pltpu.CompilerParams(collective_id=number, has_side_effects=True),
        cost_estimate=moved(16 * x.size),
        name="gather",
    )(x)


def scatter_kernel(p_ref, o_ref, held, got, one, two, send, recv, own_sem):
    me, sib, xn, yn = partners()
    diag = xn + yn - me
    half = p_ref.shape[1] // 2
    copy = functools.partial(remote, send, recv)
    upper, lower = pl.ds(0, half), pl.ds(half, half)
    greet((sib, xn, yn))
    beside, loads = [], []
    for i, owner in enumerate((diag, xn, yn, me)):
        beside.append(copy(i, p_ref.at[owner + sib - me], got.at[i], sib))
        loads.append(pltpu.make_async_copy(p_ref.at[owner], held.at[i], own_sem.at[i]))
        beside[i].start()
        loads[i].start()

    def pair_sum(i):
        beside[i].wait_recv()
        loads[i].wait()
        held[i] = held[i] + got[i]

    pair_sum(0)
    x0 = copy(4, held.at[0, upper], one.at[0], xn)
    x0.start()
    y0 = copy(5, held.at[0, lower], one.at[1], yn)
    y0.start()
    pair_sum(1)
    x1 = copy(6, held.at[1, upper], one.at[2], xn)
    x1.start()
    pair_sum(2)
    y1 = copy(7, held.at[2, lower], one.at[3], yn)
    y1.start()
    pair_sum(3)
    x0.wait_recv()
    held[2, :half] = held[2, :half] + one[0]
    y2 = copy(8, held.at[2, upper], two.at[0], yn)
    y2.start()
    y0.wait_recv()
    held[1, half:] = held[1, half:] + one[1]
    x2 = copy(9, held.at[1, lower], two.at[1], xn)
    x2.start()
    x1.wait_recv()
    y1.wait_recv()
    y2.wait_recv()
    wide = jnp.float32
    o_ref[:half] = held[3, :half].astype(wide) + one[2].astype(wide) + two[0].astype(wide)
    x2.wait_recv()
    o_ref[half:] = held[3, half:].astype(wide) + one[3].astype(wide) + two[1].astype(wide)
    for c in (*beside, x0, y0, x1, y1, y2, x2):
        c.wait_send()


def scatter_plane(part, number):
    pieces, rows, columns = part.shape
    if pieces != 8:
        return lax.psum_scatter(part, "seq", scatter_dimension=0).astype(jnp.float32)
    return pl.pallas_call(
        scatter_kernel,
        out_shape=jax.ShapeDtypeStruct((rows, columns), jnp.float32),
        in_specs=[pl.BlockSpec(memory_space=pl.ANY)],
        out_specs=pl.BlockSpec(memory_space=pltpu.VMEM),
        scratch_shapes=[
            pltpu.VMEM((4, rows, columns), LOW),
            pltpu.VMEM((4, rows, columns), LOW),
            pltpu.VMEM((4, rows // 2, columns), LOW),
            pltpu.VMEM((2, rows // 2, columns), LOW),
            pltpu.SemaphoreType.DMA((10,)),
            pltpu.SemaphoreType.DMA((10,)),
            pltpu.SemaphoreType.DMA((4,)),
        ],
        compiler_params=pltpu.CompilerParams(
            collective_id=number, has_side_effects=True, vmem_limit_bytes=40 * MIB
        ),
        cost_estimate=moved(2 * part.size),
        name="scatter",
    )(part)


def exchange_kernel(x_ref, o_ref, send, recv, own_sem):
    me = lax.axis_index("seq")
    others = [lax.rem(me + i, 8) for i in range(1, 8)]
    greet(others)
    own = pltpu.make_async_copy(x_ref.at[me], o_ref.at[me], own_sem)
    own.start()
    copies = [
        remote(send, recv, i, x_ref.at[other], o_ref.at[me], other)
        for i, other in enumerate(others)
    ]
    for c in copies:
        c.start()
    own.wait()
    for c in copies:
        c.wait()


def exchange_plane(x, number):
    if lax.axis_size("seq") != 8:
        return lax.all_to_all(x, "seq", 0, 0)
    return pl.pallas_call(
        exchange_kernel,
        out_shape=jax.ShapeDtypeStruct(x.shape, x.dtype),
        in_specs=[pl.BlockSpec(memory_space=pl.ANY)],
        out_specs=pl.BlockSpec(memory_space=pl.ANY),
        scratch_shapes=[
            pltpu.SemaphoreType.DMA((7,)),
            pltpu.SemaphoreType.DMA((7,)),
            pltpu.SemaphoreType.DMA,
        ],
        compiler_params=pltpu.CompilerParams(collective_id=number, has_side_effects=True),
        cost_estimate=moved(4 * x.size),
        name="exchange",
    )(x)


CHUNKS = (64, 64, 48)


class PlaneGather:
    def __init__(self, source, target, send, recv):
        me, sib, xn, yn = partners()
        diag = xn + yn - me
        half = target.shape[1] // 2
        upper, lower = pl.ds(0, half), pl.ds(half, half)
        copy = functools.partial(remote, send, recv)

        def direct(k, part, to):
            return copy(k, source.at[part], target.at[me, part], to)

        def pass_on(k, origin, part, to):
            return copy(k, target.at[origin, part], target.at[origin, part], to)

        self.xa, self.yb = direct(0, upper, xn), direct(1, lower, yn)
        self.xb, self.ya = direct(2, lower, xn), direct(3, upper, yn)
        self.s0 = copy(4, source, target.at[me], sib)
        self.fy, self.fx = pass_on(5, xn, upper, yn), pass_on(6, yn, lower, xn)
        self.s1, self.s2 = pass_on(7, xn, upper, sib), pass_on(8, yn, lower, sib)
        self.s3, self.s4 = pass_on(9, xn, lower, sib), pass_on(10, yn, upper, sib)
        self.s5, self.s6 = pass_on(11, diag, upper, sib), pass_on(12, diag, lower, sib)

    def start(self):
        for c in (self.xa, self.yb, self.xb, self.ya, self.s0):
            c.start()

    def forward_first(self):
        self.xa.wait_recv()
        self.yb.wait_recv()
        for c in (self.fy, self.fx, self.s1, self.s2):
            c.start()

    def forward_second(self):
        self.xb.wait_recv()
        self.ya.wait_recv()
        self.s3.start()
        self.s4.start()

    def forward_third(self):
        self.fy.wait_recv()
        self.fx.wait_recv()
        self.s5.start()
        self.s6.start()

    def from_sibling(self, chip):
        for c in {"own": (self.s0,), "x": (self.s1, self.s3), "y": (self.s2, self.s4), "diag": (self.s5, self.s6)}[chip]:
            c.wait_recv()

    def sent(self):
        for c in (self.xa, self.yb, self.xb, self.ya, self.s0, self.fy, self.fx):
            c.wait_send()
        for c in (self.s1, self.s2, self.s3, self.s4, self.s5, self.s6):
            c.wait_send()

    def arrive(self, step):
        @pl.when(step == 1)
        def _():
            self.from_sibling("own")

        @pl.when(step == 2)
        def _():
            self.forward_first()
            self.forward_second()
            self.from_sibling("x")

        @pl.when(step == 4)
        def _():
            self.from_sibling("y")

        @pl.when(step == 6)
        def _():
            self.forward_third()
            self.from_sibling("diag")


class LineGather:
    def __init__(self, item, source, block, send, recv, local=None):
        z = lax.axis_index("dp")
        self.z = z

        def copy(k, src, owner, to):
            return pltpu.make_async_remote_copy(
                src_ref=src,
                dst_ref=block(owner),
                send_sem=send.at[item, k],
                recv_sem=recv.at[item, owner],
                device_id={"dp": to},
                device_id_type=MESH,
            )

        self.sends = []
        for k, d in enumerate((2, -2, 1, -1)):
            to = z + d
            valid = (to >= 0) & (to < 4)
            self.sends.append((valid, copy(k, source, z, jnp.clip(to, 0, 3))))
        inner = (z == 1) | (z == 2)
        far = jnp.where(z == 1, 3, 0)
        self.stop = (inner, copy(4, block(far), far, jnp.where(z == 1, 0, 3)))
        others = [lax.rem(z + o, 4) for o in (1, 2, 3)]
        self.blocks = [copy(0, source, other, other) for other in others]
        self.own = None
        if local is not None:
            self.own = pltpu.make_async_copy(source, block(z), local.at[item])

    def start_far(self):
        if self.own is not None:
            self.own.start()
        self.begin(self.sends[:2])

    def start_near(self):
        self.begin(self.sends[2:])

    def start(self):
        self.start_far()
        self.start_near()

    def begin(self, sends):
        for valid, c in sends:

            @pl.when(valid)
            def _(c=c):
                c.start()

    def forward(self):
        inner, c = self.stop

        @pl.when(inner)
        def _():
            self.blocks[1].wait_recv()
            c.start()

    def wait(self):
        inner, unused = self.stop
        self.blocks[0].wait_recv()
        self.blocks[2].wait_recv()

        @pl.when(jnp.logical_not(inner))
        def _():
            self.blocks[1].wait_recv()

        if self.own is not None:
            self.own.wait()

    def sent(self):
        for valid, c in (*self.sends, self.stop):

            @pl.when(valid)
            def _(c=c):
                c.wait_send()


def nearest_first(step):
    me, sib, xn, yn = partners()
    chip = jnp.where(step < 4, xn, jnp.where(step < 6, yn, xn + yn - me))
    later = chip + jnp.where(lax.rem(step, 2) == 0, sib - me, 0)
    return jnp.where(step == 0, me, jnp.where(step == 1, sib, later))


def farthest_first(step):
    me, sib, xn, yn = partners()
    chip = jnp.where(step < 4, xn, yn)
    chip = jnp.where(step < 2, xn + yn - me, jnp.where(step < 6, chip, me))
    return chip + jnp.where(lax.rem(step, 2) == 0, sib - me, 0)


def first_of(lengths, stream, base, count):
    row = base + lax.broadcasted_iota(jnp.int32, (count, 1), 0)
    start, first = jnp.int32(0), jnp.zeros((count, 1), jnp.int32)
    for j in range(lengths.shape[1]):
        first = jnp.where(row >= start, start, first)
        start = start + lengths[stream, j]
    return first


def layer_kernel(
    x_ref,
    c_ref,
    wq_ref,
    wk_ref,
    wv_ref,
    wo_ref,
    wg_ref,
    wu_ref,
    wd_ref,
    gain_ref,
    lengths_ref,
    x_all,
    c_all,
    h2_all,
    wo_all,
    h1_out,
    q_out,
    k_out,
    v_out,
    att_out,
    tok_out,
    mid_out,
    wa_out,
    gain_out,
    out_part,
    gh_out,
    dgu_first,
    dd_first,
    dgu_out,
    dd_out,
    dgu_all,
    dd_all,
    wa,
    wgu,
    wd,
    gains,
    q_s,
    k_s,
    v_s,
    att_s,
    tok,
    mid,
    act_s,
    ggu_s,
    sum_gu,
    sum_d,
    x_buf,
    c_buf,
    o_buf,
    beside,
    held,
    got,
    one,
    two,
    gsend,
    grecv,
    zsend,
    zrecv,
    zlocal,
    esend,
    erecv,
    rsend,
    rrecv,
    load_sem,
    out_sem,
    h1_sem,
    w_sem,
    done_sem,
    self_sem,
    fsend,
    frecv,
    f_sem,
    cut_sem,
    gu_stop,
    d_stop,
):
    me, sib, xn, yn = partners()
    z = lax.axis_index("dp")
    rows, width = x_ref.shape
    span = rows // 2
    wide, qk = v_s.shape[2], q_s.shape[2]
    share = CHUNKS[0] + CHUNKS[1] + CHUNKS[2]
    half = rows // 2
    upper, lower = pl.ds(0, half), pl.ds(half, half)

    barrier = pltpu.get_barrier_semaphore()
    for i in range(1, 8):
        pl.semaphore_signal(
            barrier, inc=1, device_id={"seq": lax.rem(me + i, 8)}, device_id_type=MESH
        )
    for i in range(1, 4):
        pl.semaphore_signal(
            barrier, inc=1, device_id={"dp": lax.rem(z + i, 4)}, device_id_type=MESH
        )
    pl.semaphore_wait(barrier, 10)

    tokens = PlaneGather(x_ref, x_all, gsend.at[0], grecv.at[0])
    out_w = PlaneGather(wo_all.at[me], wo_all, gsend.at[1], grecv.at[1])
    cots = PlaneGather(c_ref, c_all, gsend.at[2], grecv.at[2])
    hidden_in = PlaneGather(held.at[0], h2_all, gsend.at[3], grecv.at[3])

    def line(item, source, block):
        return LineGather(item, source, block, zsend, zrecv, zlocal)

    def line_in_place(item, block):
        return LineGather(item, block(z), block, zsend, zrecv)

    depth = wq_ref.shape[0]

    def rows_of(ref, count, columns=None):
        def block(owner):
            if columns is None:
                return ref.at[pl.ds(owner * count, count)]
            return ref.at[pl.ds(owner * count, count), columns]

        return block

    z_gain = line(
        0, gain_ref, lambda owner: gains.at[:, pl.ds(pl.multiple_of(owner * depth, 128), depth)]
    )
    z_attn = line_in_place(1, rows_of(wa, depth))
    z_out = line(
        2,
        wo_ref.at[:, pl.ds(pl.multiple_of(me * wide, 128), wide)],
        lambda owner: wo_all.at[me, pl.ds(owner * depth, depth)],
    )
    z_up, z_down = [], []
    column, before = 0, 0
    columns, hiddens = [], []
    for k, count in enumerate(CHUNKS):
        part = pl.ds(column, 8 * count)
        z_up.append(line_in_place(3 + k, rows_of(wgu, depth, part)))
        z_down.append(
            line(
                6 + k,
                wd_ref.at[pl.ds(me * share + before, count)],
                lambda owner, base=4 * before, count=count: wd.at[
                    pl.ds(base + owner * count, count)
                ],
            )
        )
        columns.append(column)
        hiddens.append(4 * before)
        column += 8 * count
        before += count

    tokens.start()
    z_gain.start()

    window = 384
    tall = depth // 2

    def cut_window(i, source, start, size, r, slot, lane):
        return pltpu.make_async_copy(
            source.at[pl.ds(r * tall, tall), pl.ds(pl.multiple_of(start, 128), size)],
            got.at[slot, :, pl.ds(lane, size)],
            cut_sem.at[i],
        )

    per_tile = 128 // qk
    narrow = me // per_tile * 128
    shift = lax.rem(me, per_tile) * qk
    own_rows = pl.ds(pl.multiple_of(z * depth, depth), depth)
    v_cut = pltpu.make_async_copy(
        wv_ref.at[:, pl.ds(pl.multiple_of(me * wide, 128), wide)],
        wa.at[own_rows, pl.ds(0, wide)],
        cut_sem.at[20],
    )
    v_cut.start()
    qk_cuts = [
        cut_window(2 * r + i, source, narrow, 128, r, r, 128 * i)
        for r in range(2)
        for i, source in enumerate((wq_ref, wk_ref))
    ]
    for c in qk_cuts:
        c.start()
    ff_cuts = []
    ff_width = wg_ref.shape[1]
    for second, source in enumerate((wg_ref, wu_ref)):
        for group in range(4):
            start = group * (ff_width // 4) + me * share
            aligned = jnp.minimum(start // 128 * 128, ff_width - window)
            lane = 256 * (1 - second) + window * group
            for r in range(2):
                c = cut_window(
                    4 + len(ff_cuts), source, aligned, window, r, 2 * second + r, lane
                )
                c.start()
                ff_cuts.append((c, second, group, r, lane, start - aligned))
    for c in qk_cuts:
        c.wait()
    for r in range(2):
        lane = lax.broadcasted_iota(jnp.int32, (tall, 128), 1)
        q_rows = pltpu.roll(got[r, :, 0:128].astype(jnp.float32), lax.rem(128 - shift, 128), 1)
        k_rows = pltpu.roll(
            got[r, :, 128:256].astype(jnp.float32), lax.rem(128 + qk - shift, 128), 1
        )
        both = jnp.where(lane < qk, q_rows, jnp.where(lane < 2 * qk, k_rows, 0.0))
        there = pl.ds(pl.multiple_of(z * depth + r * tall, tall), tall)
        wa[there, wide : wide + 128] = both.astype(LOW)
    v_cut.wait()
    z_attn.start()
    for c, second, group, r, lane, shift_by in ff_cuts:
        c.wait()
        rolled = pltpu.roll(
            got[2 * second + r, :, lane : lane + window].astype(jnp.float32),
            lax.rem(window - shift_by, window),
            1,
        )
        there = pl.ds(pl.multiple_of(z * depth + r * tall, tall), tall)
        begin = 0
        for k, count in enumerate(CHUNKS):
            at = columns[k] + (4 * second + group) * count
            wgu[there, at : at + count] = rolled[:, begin : begin + count].astype(LOW)
            begin += count

    def loads(order, step, sources):
        slot = lax.rem(step, 2)
        owner = order(step)
        return [
            pltpu.make_async_copy(source.at[owner], buf.at[slot], load_sem.at[i, slot])
            for i, (source, buf) in enumerate(sources)
        ]

    first_load = pltpu.make_async_copy(x_ref, x_buf.at[0], load_sem.at[0, 0])
    first_load.start()
    own_c = pltpu.make_async_copy(c_ref, c_all.at[me], self_sem.at[3])
    own_c.start()
    tokens.forward_first()
    z_gain.forward()
    z_attn.forward()
    tokens.forward_second()
    cots.start()
    z_gain.wait()
    z_attn.wait()
    z_out.start()

    def h1_copies(step):
        slot = lax.rem(step, 2)
        owner = nearest_first(step)
        return [
            pltpu.make_async_copy(
                o_buf.at[slot, pl.ds(m * span, span)],
                h1_out.at[m, pl.ds(owner * span, span)],
                h1_sem.at[m, slot],
            )
            for m in range(2)
        ]

    def arrive_tokens(step):
        @pl.when(step == 1)
        def _():
            tokens.from_sibling("own")

        @pl.when(step == 2)
        def _():
            tokens.from_sibling("x")

        @pl.when(step == 4)
        def _():
            tokens.forward_third()
            tokens.from_sibling("y")

        @pl.when(step == 3)
        def _():
            for g in (z_up[0], z_down[0]):
                g.start()

        @pl.when(step == 6)
        def _():
            tokens.from_sibling("diag")

        @pl.when(step == 7)
        def _():
            z_out.forward()

    token_source = [(x_all, x_buf)]

    def project(step, carry):
        slot = lax.rem(step, 2)
        owner = nearest_first(step)
        for c in loads(nearest_first, step, token_source):
            c.wait()

        @pl.when(step >= 2)
        def _():
            for c in h1_copies(step - 2):
                c.wait()

        x = x_buf[slot].astype(jnp.float32)
        gain = gains[0:1, :].astype(jnp.float32)
        h_one = (x * norm_scale(x) * gain).astype(LOW)
        o_buf[slot] = h_one
        for c in h1_copies(step):
            c.start()
        arrive_tokens(step + 1)

        @pl.when(step < 7)
        def _():
            for c in loads(nearest_first, step + 1, token_source):
                c.start()

        projected = dot(h_one, wa[...]).astype(LOW)
        for m in range(2):
            there = pl.ds(owner * span, span)
            mine = projected[m * span : (m + 1) * span]
            v_s[m, there, :] = mine[:, :wide]
            q_s[m, there, :] = mine[:, wide : wide + qk]
            k_s[m, there, :] = mine[:, wide + qk : wide + 2 * qk]
        return carry

    lax.fori_loop(0, 8, project, 0)
    for step in (6, 7):
        for c in h1_copies(step):
            c.wait()
    z_out.wait()
    out_w.start()
    for g in (z_up[1], z_down[1]):
        g.start()

    finals = [
        pltpu.make_async_copy(source, target, done_sem.at[i])
        for i, (source, target) in enumerate(
            (
                (q_s, q_out),
                (k_s, k_out),
                (v_s, v_out),
                (wa, wa_out),
                (gains, gain_out),
                (att_s, att_out),
                (tok, tok_out),
                (mid, mid_out),
            )
        )
    ]
    for c in finals[:5]:
        c.start()

    length = v_s.shape[1]
    block = 256

    def attend_stream(m, carry):
        for i in range(length // block):
            rows_i = slice(i * block, (i + 1) * block)
            seen = (i + 1) * block
            first = first_of(lengths_ref, m, i * block, block)
            for head in range(wide // HEAD_V):
                lanes = slice(head * HEAD_V, (head + 1) * HEAD_V)
                unused, unused_mask, weight = weights_of(
                    q_s[m, rows_i, :], k_s[m, :seen, :], head, first, i * block
                )
                denom = jnp.sum(weight, axis=1, keepdims=True)
                numer = dot(weight.astype(LOW), v_s[m, :seen, lanes])
                att_s[m, rows_i, lanes] = (numer / denom).astype(LOW)
        return carry

    lax.fori_loop(0, 2, attend_stream, 0)
    out_w.forward_first()
    finals[5].start()

    to_mine = pl.ds(pl.multiple_of(me * wide, 128), wide)
    swaps = []
    for i in range(1, 8):
        other = lax.rem(me + i, 8)
        for m in range(2):
            swaps.append(
                remote(
                    esend,
                    erecv,
                    2 * (i - 1) + m,
                    att_s.at[m, pl.ds(other * span, span)],
                    tok.at[pl.ds(m * span, span), to_mine],
                    other,
                )
            )
            swaps[-1].start()
    kept = [
        pltpu.make_async_copy(
            att_s.at[m, pl.ds(me * span, span)],
            tok.at[pl.ds(m * span, span), to_mine],
            self_sem.at[m],
        )
        for m in range(2)
    ]
    for c in kept:
        c.start()
    x_load = pltpu.make_async_copy(x_ref, x_buf.at[0], load_sem.at[0, 0])
    x_load.start()

    def w_lanes(slot):
        return pl.ds(pl.multiple_of(slot * wide, 128), wide)

    def w_load(step):
        slot = lax.rem(step, 2)
        return pltpu.make_async_copy(
            wo_all.at[nearest_first(step)], act_s.at[:, w_lanes(slot)], w_sem.at[slot]
        )

    w_load(0).start()
    out_w.forward_second()
    cots.forward_first()
    cots.forward_second()
    z_up[0].forward()
    z_down[0].forward()
    for g in (z_up[2], z_down[2]):
        g.start_far()
    for c in kept:
        c.wait()
    for c in swaps:
        c.wait_recv()
    finals[6].start()
    x_load.wait()

    def arrive_out(step):
        @pl.when(step == 1)
        def _():
            out_w.from_sibling("own")

        @pl.when(step == 2)
        def _():
            out_w.from_sibling("x")

        @pl.when(step == 4)
        def _():
            out_w.forward_third()
            out_w.from_sibling("y")

        @pl.when(step == 6)
        def _():
            out_w.from_sibling("diag")

    def project_out(step, carry):
        slot = lax.rem(step, 2)
        owner = nearest_first(step)
        w_load(step).wait()
        arrive_out(step + 1)

        @pl.when(step < 7)
        def _():
            w_load(step + 1).start()

        there = pl.ds(pl.multiple_of(owner * wide, 128), wide)
        mid[:, there] = dot(tok[...], act_s[:, w_lanes(slot)])
        return carry

    lax.fori_loop(0, 8, project_out, 0)
    mid_value = x_buf[0].astype(jnp.float32) + mid[...]
    mid[...] = mid_value
    held[0] = (mid_value * norm_scale(mid_value) * gains[1:2, :].astype(jnp.float32)).astype(LOW)
    hidden_in.start()
    own_h2 = pltpu.make_async_copy(held.at[0], h2_all.at[me], self_sem.at[2])
    own_h2.start()
    for g in (z_up[2], z_down[2]):
        g.start_near()
    cots.forward_third()
    own_h2.wait()
    own_c.wait()
    z_up[0].wait()
    z_down[0].wait()

    largest = 4 * max(CHUNKS)
    sources = [(h2_all, x_buf), (c_all, c_buf)]

    def out_copy(order, step):
        slot = lax.rem(step, 2)
        return pltpu.make_async_copy(o_buf.at[slot], out_part.at[order(step)], out_sem.at[slot])

    def hidden_chunk(k, owner, h, c):
        count = 4 * CHUNKS[k]
        pair = pl.ds(columns[k], 2 * count)
        here = pl.ds(hiddens[k], count)
        both = dot(h, wgu[:, pair])
        gate, up = both[:, :count], both[:, count:]
        g_act = contract(c, wd[here, :], 1, 1)
        sigmoid = jax.nn.sigmoid(gate)
        silu = gate * sigmoid
        act = (silu * up).astype(LOW)
        g_gate = (g_act * up * sigmoid * (1.0 + gate * (1.0 - sigmoid))).astype(LOW)
        g_up = (g_act * silu).astype(LOW)
        there = pl.ds(owner * rows, rows)
        act_s[there, here] = act
        g_both = jnp.concatenate([g_gate, g_up], axis=1)
        ggu_s[there, pair] = g_both
        return act, g_both

    def add_grads(k, step, h, c, act, g_both):
        count = 4 * CHUNKS[k]

        to, low = (2 * largest, largest) if k == 1 else (0, 0)

        @pl.when(step == 0)
        def _():
            sum_gu[:, to : to + 2 * count] = jnp.zeros((width, 2 * count), jnp.float32)
            sum_d[low : low + count, :] = jnp.zeros((count, width), jnp.float32)

        sum_gu[:, to : to + 2 * count] += contract(h, g_both, 0, 0)
        sum_d[low : low + count, :] += contract(act, c, 0, 0)

    def emit(k):
        count = 4 * CHUNKS[k]
        rest = share - CHUNKS[0]
        to, low = (2 * largest, largest) if k == 1 else (0, 0)

        def gu_copies(i, slot):
            there = pl.ds(i * rows, rows)
            if k == 0:
                return [
                    pltpu.make_async_copy(
                        o_buf.at[slot, :, pl.ds(second * count, count)],
                        dgu_first.at[second, there],
                        h1_sem.at[second, slot],
                    )
                    for second in range(2)
                ]
            return [
                pltpu.make_async_copy(
                    o_buf.at[slot, :, pl.ds(0, 2 * count)],
                    dgu_out.at[there, pl.ds(columns[k] - columns[1], 2 * count)],
                    out_sem.at[slot],
                )
            ]

        def d_target(owner):
            if k == 0:
                return dd_first.at[pl.ds(owner * CHUNKS[0], CHUNKS[0])]
            start = owner * rest + (hiddens[k] - hiddens[1]) // 4
            return dd_out.at[pl.ds(start, CHUNKS[k])]

        pending = [[], []]
        for i in range(width // rows):
            slot = i % 2
            for c in pending[slot]:
                c.wait()
            total = sum_gu[i * rows : (i + 1) * rows, to : to + 2 * count]
            o_buf[slot, :, : 2 * count] = total.astype(LOW)
            pending[slot] = gu_copies(i, slot)
            for c in pending[slot]:
                c.start()
        for c in (*pending[0], *pending[1]):
            c.wait()
        o_buf[0, :count, :] = sum_d[low : low + count, :].astype(LOW)
        downs = []
        for owner in range(4):
            downs.append(
                pltpu.make_async_copy(
                    o_buf.at[0, pl.ds(owner * CHUNKS[k], CHUNKS[k])],
                    d_target(owner),
                    h1_sem.at[owner // 2, owner % 2],
                )
            )
            downs[-1].start()
        for c in downs:
            c.wait()

    def forward_pass(chunks, last, arrive, step, carry):
        slot = lax.rem(step, 2)
        for c in loads(nearest_first, step, sources):
            c.wait()
        h, c = x_buf[slot], c_buf[slot]
        made = [hidden_chunk(k, nearest_first(step), h, c) for k in chunks]
        if arrive is not None:
            arrive(step + 1)

        @pl.when(step < last)
        def _():
            for c in loads(nearest_first, step + 1, sources):
                c.start()

        for k, (act, g_both) in zip(chunks, made):
            add_grads(k, step, h, c, act, g_both)
        return carry

    def arrive_both(step):
        hidden_in.arrive(step)

        @pl.when(step == 1)
        def _():
            cots.from_sibling("own")

        @pl.when(step == 2)
        def _():
            cots.from_sibling("x")

        @pl.when(step == 4)
        def _():
            cots.from_sibling("y")

        @pl.when(step == 6)
        def _():
            cots.from_sibling("diag")

        @pl.when(step == 7)
        def _():
            z_up[2].forward()
            z_down[2].forward()

    for c in loads(nearest_first, 0, sources):
        c.start()

    def arrive_near(step):
        @pl.when(step < 4)
        def _():
            arrive_both(step)

    lax.fori_loop(0, 4, functools.partial(forward_pass, (0,), 3, arrive_near), 0)
    for c in loads(nearest_first, 0, sources):
        c.start()
    z_up[1].forward()
    z_down[1].forward()
    z_up[1].wait()
    z_down[1].wait()
    lax.fori_loop(0, 4, functools.partial(forward_pass, (1,), 3, None), 0)
    arrive_both(jnp.int32(4))
    for c in loads(nearest_first, 4, sources):
        c.start()
    lax.fori_loop(4, 8, functools.partial(forward_pass, (0, 1), 7, arrive_both), 0)
    hidden_in.sent()
    finals[7].start()
    for c in loads(farthest_first, 0, sources):
        c.start()
    emit(0)
    sum_lines = [
        LineScatter(
            lambda owner: dgu_first.at[:, pl.ds(owner * depth, depth), :],
            dgu_all,
            gu_stop,
            att_s.at[:, pl.ds(0, depth), :],
            fsend.at[0],
            frecv.at[0],
            f_sem.at[0],
        ),
        LineScatter(
            lambda owner: dd_first.at[pl.ds(owner * CHUNKS[0], CHUNKS[0])],
            dd_all,
            d_stop,
            tok.at[pl.ds(0, CHUNKS[0])],
            fsend.at[1],
            frecv.at[1],
            f_sem.at[1],
        ),
    ]
    for c in swaps:
        c.wait_send()
    finals[5].wait()
    finals[6].wait()
    for g in sum_lines:
        g.start_first()

    z_up[2].wait()
    z_down[2].wait()

    copy = functools.partial(remote, rsend, rrecv)
    b_diag = copy(0, beside.at[0], got.at[2], sib)
    b_x = copy(1, beside.at[1], got.at[1], sib)
    b_y = copy(2, beside.at[0], got.at[3], sib)
    b_own = copy(3, beside.at[1], got.at[0], sib)
    x0 = copy(4, held.at[2, upper], one.at[0], xn)
    y0 = copy(5, held.at[2, lower], one.at[1], yn)
    x1 = copy(6, held.at[1, upper], one.at[2], xn)
    y1 = copy(7, held.at[3, lower], one.at[3], yn)
    y2 = copy(8, held.at[3, upper], two.at[0], yn)
    x2 = copy(9, held.at[1, lower], two.at[1], xn)

    def last_pass(step, carry):
        slot = lax.rem(step, 2)
        owner = farthest_first(step)
        there = pl.ds(owner * rows, rows)
        for c in loads(farthest_first, step, sources):
            c.wait()
        hidden_chunk(2, owner, x_buf[slot], c_buf[slot])

        @pl.when(step < 7)
        def _():
            for c in loads(farthest_first, step + 1, sources):
                c.start()

        part = contract(ggu_s[there, :], wgu[...], 1, 1).astype(LOW)

        @pl.when(step == 2)
        def _():
            for g in sum_lines:
                g.start()

        @pl.when(step == 6)
        def _():
            for g in sum_lines:
                g.join()

        for k, place, sent in ((0, 0, b_diag), (2, 1, b_x), (4, 0, b_y), (6, 1, b_own)):

            @pl.when(step == k)
            def _(k=k, place=place, sent=sent):
                if k == 4:
                    b_diag.wait_send()
                if k == 6:
                    b_x.wait_send()
                beside[place] = part
                sent.start()

        for k, place, arrived in ((1, 2, b_diag), (3, 1, b_x), (5, 3, b_y), (7, 0, b_own)):

            @pl.when(step == k)
            def _(k=k, place=place, arrived=arrived):
                arrived.wait_recv()
                held[place] = part + got[place]
                if k == 1:
                    x0.start()
                    y0.start()
                if k == 3:
                    x1.start()
                if k == 5:
                    y1.start()
                    y0.wait_recv()
                    held[1, half:] = held[1, half:] + one[1]
                    x2.start()
                    x0.wait_recv()
                    held[3, :half] = held[3, :half] + one[0]
                    y2.start()
        return carry

    lax.fori_loop(0, 8, last_pass, 0)
    for c in loads(farthest_first, 0, sources):
        c.start()

    def close_pass(step, carry):
        slot = lax.rem(step, 2)
        there = pl.ds(farthest_first(step) * rows, rows)
        for c in loads(farthest_first, step, sources):
            c.wait()

        @pl.when(step < 7)
        def _():
            for c in loads(farthest_first, step + 1, sources):
                c.start()

        @pl.when(step >= 2)
        def _():
            out_copy(farthest_first, step - 2).wait()

        o_buf[slot] = dot(act_s[there, :], wd[...]).astype(LOW)
        out_copy(farthest_first, step).start()
        act = act_s[there, pl.ds(hiddens[2], 4 * CHUNKS[2])]
        g_both = ggu_s[there, pl.ds(columns[2], 8 * CHUNKS[2])]
        add_grads(2, step, x_buf[slot], c_buf[slot], act, g_both)
        return carry

    lax.fori_loop(0, 8, close_pass, 0)
    out_copy(farthest_first, 6).wait()
    out_copy(farthest_first, 7).wait()
    emit(1)
    emit(2)
    f32 = jnp.float32
    x1.wait_recv()
    y2.wait_recv()
    for c in (*finals[:5], finals[7]):
        c.wait()
    mid[:half] = held[0, :half].astype(f32) + one[2].astype(f32) + two[0].astype(f32)
    y1.wait_recv()
    x2.wait_recv()
    mid[half:] = held[0, half:].astype(f32) + one[3].astype(f32) + two[1].astype(f32)
    gh_copy = pltpu.make_async_copy(mid, gh_out, done_sem.at[7])
    gh_copy.start()
    for g in sum_lines:
        g.wait()
    gh_copy.wait()
    for c in (b_y, b_own, x0, y0, x1, y1, y2, x2):
        c.wait_send()
    for g in (tokens, out_w, cots, z_gain, z_attn, z_out, *z_up, *z_down):
        g.sent()


def layer_front(tokens, cot, weights, gain_rows, lengths, length, wide, qk):
    rows, width = tokens.shape
    streams = lengths.shape[0]
    hidden = 4 * sum(CHUNKS)
    largest = 4 * max(CHUNKS)
    shape = jax.ShapeDtypeStruct
    f32 = jnp.float32
    anywhere = pl.BlockSpec(memory_space=pl.ANY)
    plane = shape((8, rows, width), LOW)
    narrow = shape((streams, length, qk), LOW)
    broad = shape((streams, length, wide), LOW)
    attn_shape = (width, wide + 128)
    out_shape = [
        plane,
        plane,
        plane,
        shape((8, width, width // 8), LOW),
        shape((streams, length, width), LOW),
        narrow,
        narrow,
        broad,
        broad,
        shape((rows, width), LOW),
        shape((rows, width), f32),
        shape(attn_shape, LOW),
        shape((gain_rows.shape[0], width), LOW),
        plane,
        shape((rows, width), f32),
        shape((2, width, 4 * CHUNKS[0]), LOW),
        shape((4 * CHUNKS[0], width), LOW),
        shape((width, 2 * hidden - 8 * CHUNKS[0]), LOW),
        shape((hidden - 4 * CHUNKS[0], width), LOW),
        shape((4, 2, width // 4, 4 * CHUNKS[0]), LOW),
        shape((4, CHUNKS[0], width), LOW),
    ]
    dma = pltpu.SemaphoreType.DMA
    vmem = pltpu.VMEM
    return pl.pallas_call(
        layer_kernel,
        out_shape=out_shape,
        in_specs=[anywhere] * 10 + [pl.BlockSpec(memory_space=pltpu.SMEM)],
        out_specs=[anywhere] * 21,
        scratch_shapes=[
            vmem(attn_shape, LOW),
            vmem((width, 2 * hidden), LOW),
            vmem((hidden, width), LOW),
            vmem((gain_rows.shape[0], width), LOW),
            vmem(narrow.shape, LOW),
            vmem(narrow.shape, LOW),
            vmem(broad.shape, LOW),
            vmem(broad.shape, LOW),
            vmem((rows, width), LOW),
            vmem((rows, width), f32),
            vmem((8 * rows, hidden), LOW),
            vmem((8 * rows, 2 * hidden), LOW),
            vmem((width, 4 * largest), f32),
            vmem((2 * largest, width), f32),
            vmem((2, rows, width), LOW),
            vmem((2, rows, width), LOW),
            vmem((2, rows, width), LOW),
            vmem((2, rows, width), LOW),
            vmem((4, rows, width), LOW),
            vmem((4, rows, width), LOW),
            vmem((4, rows // 2, width), LOW),
            vmem((2, rows // 2, width), LOW),
            dma((4, 13)),
            dma((4, 13)),
            dma((9, 5)),
            dma((9, 4)),
            dma((9,)),
            dma((14,)),
            dma((14,)),
            dma((10,)),
            dma((10,)),
            dma((2, 2)),
            dma((2,)),
            dma((2, 2)),
            dma((2,)),
            dma((8,)),
            dma((4,)),
            dma((2, 5)),
            dma((2, 5)),
            dma((2, 2)),
            dma((21,)),
            vmem((2, width // 4, 4 * CHUNKS[0]), LOW),
            vmem((CHUNKS[0], width), LOW),
        ],
        compiler_params=pltpu.CompilerParams(
            collective_id=21, has_side_effects=True, vmem_limit_bytes=63 * MIB
        ),
        cost_estimate=pl.CostEstimate(
            flops=6 * 3 * 8 * rows * width * hidden,
            bytes_accessed=400 * rows * width,
            transcendentals=0,
        ),
        name="layer",
    )(tokens, cot, *weights, gain_rows, lengths)


class LineScatter:
    def __init__(self, block, target, stop, mine, send, recv, local):
        z = lax.axis_index("dp")
        self.z, self.stop, self.mine = z, stop, mine
        self.inner = (z == 1) | (z == 2)
        self.outer = jnp.logical_not(self.inner)

        def copy(k, src, dst, at, to):
            return pltpu.make_async_remote_copy(
                src_ref=src,
                dst_ref=dst,
                send_sem=send.at[k],
                recv_sem=recv.at[at],
                device_id={"dp": to},
                device_id_type=MESH,
            )

        far = jnp.where(z < 2, 3, 0)
        near = jnp.where(z < 2, 1, 2)
        self.first = copy(0, block(far), stop, 4, jnp.where(self.inner, 3 - near, near))
        self.sends = []
        for k, d in enumerate((1, -1)):
            to = z + d
            valid = (to >= 0) & (to < 4)
            there = jnp.clip(to, 0, 3)
            self.sends.append((valid, copy(1 + k, block(there), target.at[z], z, there)))
        other = 3 - near
        self.sends.append((self.outer, copy(3, block(other), target.at[z], z, other)))
        self.own_far = pltpu.make_async_copy(block(far), mine, local.at[0])
        self.joined = copy(4, mine, target.at[z], z, far)
        self.own = pltpu.make_async_copy(block(z), target.at[z], local.at[1])
        self.arrivals = []
        for d in (1, -1, 2, -2):
            owner = z + d
            valid = (owner >= 0) & (owner < 4)
            there = jnp.clip(owner, 0, 3)
            self.arrivals.append((valid, copy(1, block(there), target.at[there], there, there)))

    def start_first(self):
        self.own.start()

        @pl.when(self.outer)
        def _():
            self.first.start()

        @pl.when(self.inner)
        def _():
            self.own_far.start()

    def start(self):
        for valid, c in self.sends:

            @pl.when(valid)
            def _(c=c):
                c.start()

    def join(self):
        @pl.when(self.inner)
        def _():
            self.first.wait_recv()
            self.own_far.wait()
            self.mine[...] = self.mine[...] + self.stop[...]
            self.joined.start()

    def wait(self):
        for valid, c in self.arrivals:

            @pl.when(valid)
            def _(c=c):
                c.wait_recv()

        self.own.wait()
        for valid, c in (*self.sends, (self.outer, self.first), (self.inner, self.joined)):

            @pl.when(valid)
            def _(c=c):
                c.wait_send()


class PlaneScatter:
    def __init__(self, beside, held, got, one, two, send, recv):
        me, sib, xn, yn = partners()
        half = got.shape[1] // 2
        self.half = half
        upper, lower = pl.ds(0, half), pl.ds(half, half)
        copy = functools.partial(remote, send, recv)
        self.held, self.got, self.one, self.two = held, got, one, two
        self.pairs = [copy(i, beside(i), got.at[i], sib) for i in range(4)]
        self.x0 = copy(4, held(2).at[upper], one.at[0], xn)
        self.y0 = copy(5, held(2).at[lower], one.at[1], yn)
        self.x1 = copy(6, held(1).at[upper], one.at[2], xn)
        self.y1 = copy(7, held(3).at[lower], one.at[3], yn)
        self.y2 = copy(8, held(3).at[upper], two.at[0], yn)
        self.x2 = copy(9, held(1).at[lower], two.at[1], xn)

    def start_pair(self, i):
        self.pairs[i].start()

    def start_pairs(self):
        for i in (2, 1, 3, 0):
            self.start_pair(i)

    def add_pair(self, i):
        self.pairs[i].wait_recv()
        block = self.held(i)
        block[...] = block[...] + self.got[i]
        for c in {0: (), 1: (self.x1,), 2: (self.x0, self.y0), 3: (self.y1,)}[i]:
            c.start()

    def add_pairs(self):
        for i in (2, 1, 3, 0):
            self.add_pair(i)

    def second(self):
        half = self.half
        self.y0.wait_recv()
        block = self.held(1)
        block[half:, :] = block[half:, :] + self.one[1]
        self.x2.start()
        self.x0.wait_recv()
        block = self.held(3)
        block[:half, :] = block[:half, :] + self.one[0]
        self.y2.start()

    def upper_sum(self):
        f32 = jnp.float32
        self.x1.wait_recv()
        self.y2.wait_recv()
        own = self.held(0)[: self.half, :].astype(f32)
        return own + self.one[2].astype(f32) + self.two[0].astype(f32)

    def lower_sum(self):
        f32 = jnp.float32
        self.y1.wait_recv()
        self.x2.wait_recv()
        own = self.held(0)[self.half :, :].astype(f32)
        return own + self.one[3].astype(f32) + self.two[1].astype(f32)

    def sent(self):
        for c in (*self.pairs, self.x0, self.y0, self.x1, self.y1, self.y2, self.x2):
            c.wait_send()


def chips():
    me, unused, xn, yn = partners()
    return me, xn, xn + yn - me, yn


def turn_kernel(
    gh_ref,
    mid_ref,
    c_ref,
    gain_ref,
    wo_all,
    part_ref,
    tok_ref,
    q_ref,
    k_ref,
    v_ref,
    att_ref,
    lengths_ref,
    h1_ref,
    output_ref,
    g_mid_out,
    g_out,
    gain_out,
    attn_ref,
    g_mid,
    work,
    g_low,
    g_att,
    g_heads,
    g_s,
    w_buf,
    go_part,
    held_o,
    got_g,
    one_g,
    two_g,
    got_o,
    one_o,
    two_o,
    gk_sum,
    gv_sum,
    h_buf,
    sums,
    esend,
    erecv,
    ssend,
    srecv,
    load_sem,
    w_sem,
    self_sem,
    done_sem,
    h_sem,
):
    me, sib, xn, yn = partners()
    flip = sib - me
    rows, width = g_low.shape
    span = rows // 2
    wide, qk = v_ref.shape[2], q_ref.shape[2]
    half = rows // 2
    greet([lax.rem(me + i, 8) for i in range(1, 8)])
    owners = chips()

    loads = [
        pltpu.make_async_copy(source, target, load_sem.at[i])
        for i, (source, target) in enumerate(
            ((gh_ref, g_mid), (mid_ref, work), (c_ref, g_low))
        )
    ]
    held_loads = [
        pltpu.make_async_copy(part_ref.at[owners[i]], held_o.at[i], load_sem.at[3 + i])
        for i in range(4)
    ]

    def w_load(step):
        slot = lax.rem(step, 2)
        return pltpu.make_async_copy(wo_all.at[step], w_buf.at[slot], w_sem.at[slot])

    for c in loads:
        c.start()
    w_load(0).start()
    outs = PlaneScatter(
        lambda i: part_ref.at[owners[i] + flip],
        lambda i: held_o.at[i],
        got_o,
        one_o,
        two_o,
        ssend.at[0],
        srecv.at[0],
    )
    weights = PlaneScatter(
        lambda i: go_part.at[owners[i] + flip],
        lambda i: go_part.at[owners[i]],
        got_g,
        one_g,
        two_g,
        ssend.at[1],
        srecv.at[1],
    )
    outs.start_pairs()
    for c in held_loads:
        c.start()
    for c in loads:
        c.wait()

    f32 = jnp.float32
    mid = work[...]
    inverse = norm_scale(mid)
    normed = mid * inverse
    grad = g_mid[...]
    gain_out[...] = jnp.broadcast_to(
        jnp.sum(grad * normed, axis=0, keepdims=True), gain_out.shape
    )
    gain = gain_ref[1:2, :].astype(f32)
    grad_mid = g_low[...].astype(f32) + norm_backward(grad, normed, inverse, gain)
    g_mid[...] = grad_mid
    g_low[...] = grad_mid.astype(LOW)
    done = [pltpu.make_async_copy(g_mid, g_mid_out, done_sem.at[0])]
    done[0].start()

    def back_out(step, carry):
        slot = lax.rem(step, 2)
        w_load(step).wait()

        @pl.when(step < 7)
        def _():
            w_load(step + 1).start()

        there = pl.ds(pl.multiple_of(step * wide, 128), wide)
        term = contract(g_low[:, there], w_buf[slot], 1, 1)

        @pl.when(step == 0)
        def _():
            work[...] = term

        @pl.when(step > 0)
        def _():
            work[...] += term

        return carry

    lax.fori_loop(0, 8, back_out, 0)
    g_att[...] = work[...].astype(LOW)
    mid_load = pltpu.make_async_copy(mid_ref, work, load_sem.at[1])
    mid_load.start()
    swaps = []
    here = pl.ds(me * span, span)
    for i in range(1, 8):
        other = lax.rem(me + i, 8)
        lanes = pl.ds(pl.multiple_of(other * wide, 128), wide)
        for m in range(2):
            swaps.append(
                remote(
                    esend,
                    erecv,
                    2 * (i - 1) + m,
                    g_att.at[pl.ds(m * span, span), lanes],
                    g_heads.at[m, here],
                    other,
                )
            )
            swaps[-1].start()
    kept = [
        pltpu.make_async_copy(
            g_att.at[pl.ds(m * span, span), pl.ds(pl.multiple_of(me * wide, 128), wide)],
            g_heads.at[m, here],
            self_sem.at[m],
        )
        for m in range(2)
    ]
    for c in kept:
        c.start()

    own = width // 32
    for z in range(4):
        lanes = slice(z * 8 * own, (z + 1) * 8 * own)
        block = contract(tok_ref[:, lanes], g_low[...], 0, 0).astype(LOW)
        for s in range(8):
            go_part[s, z * own : (z + 1) * own, :] = block[s * own : (s + 1) * own]
    weights.start_pairs()
    for c in kept:
        c.wait()
    for c in swaps:
        c.wait_recv()
    weights.add_pairs()

    length = v_ref.shape[1]
    block = 256
    streams = v_ref.shape[0]
    pieces = length // rows

    def h_load(step):
        slot = lax.rem(step, 2)
        return pltpu.make_async_copy(
            h1_ref.at[step // pieces, pl.ds(lax.rem(step, pieces) * rows, rows)],
            h_buf.at[slot],
            h_sem.at[slot],
        )

    h_load(0).start()

    def back_stream(m, carry):
        gk_sum[...] = jnp.zeros_like(gk_sum)
        gv_sum[...] = jnp.zeros_like(gv_sum)
        for i in range(length // block):
            rows_i = slice(i * block, (i + 1) * block)
            seen = (i + 1) * block
            query, key = q_ref[m, rows_i, :], k_ref[m, :seen, :]
            g_query = jnp.zeros(query.shape, f32)
            first = first_of(lengths_ref, m, i * block, block)
            for head in range(wide // HEAD_V):
                lanes = slice(head * HEAD_V, (head + 1) * HEAD_V)
                scores, mask, weight = weights_of(query, key, head, first, i * block)
                denom = jnp.sum(weight, axis=1, keepdims=True)
                a = (g_heads[m, rows_i, lanes].astype(f32) / denom).astype(LOW)
                b = -jnp.sum(
                    a.astype(f32) * att_ref[m, rows_i, lanes].astype(f32), axis=1, keepdims=True
                )
                g_weight = contract(a, v_ref[m, :seen, lanes], 1, 1) + b
                slope = 1.0 / math.sqrt(QK_DIM) + scores * (1.0 / QK_DIM)
                g_scores = jnp.where(mask, g_weight * slope, 0.0).astype(LOW)
                g_query += head_lanes(dot(g_scores, key), head)
                gk_sum[:seen, :] += contract(g_scores, head_lanes(query, head), 0, 0)
                gv_sum[:seen, lanes] += contract(weight.astype(LOW), a, 0, 0)
            g_s[m, rows_i, wide : wide + qk] = g_query.astype(LOW)
        g_s[m, :, :wide] = gv_sum[...].astype(LOW)
        g_s[m, :, wide + qk : wide + 2 * qk] = gk_sum[...].astype(LOW)
        g_s[m, :, wide + 2 * qk :] = jnp.zeros((length, g_s.shape[2] - wide - 2 * qk), LOW)

        @pl.when(m == 0)
        def _():
            for c in held_loads:
                c.wait()
            outs.add_pairs()

        return carry

    lax.fori_loop(0, 2, back_stream, 0)
    weights.second()
    done.append(pltpu.make_async_copy(g_s, g_out, done_sem.at[1]))
    done[1].start()
    outs.second()

    def add_grads(step, carry):
        slot = lax.rem(step, 2)
        h_load(step).wait()

        @pl.when(step < streams * pieces - 1)
        def _():
            h_load(step + 1).start()

        there = pl.ds(pl.multiple_of(lax.rem(step, pieces) * rows, rows), rows)
        term = contract(h_buf[slot], g_s[step // pieces, there, :], 0, 0)

        @pl.when(step == 0)
        def _():
            sums[...] = term

        @pl.when(step > 0)
        def _():
            sums[...] += term

        return carry

    lax.fori_loop(0, streams * pieces, add_grads, 0)
    narrow = sums.shape[1]
    attn_ref[:, :narrow] = sums[...].astype(LOW)
    mid_load.wait()
    for part, total in enumerate((weights.upper_sum(), weights.lower_sum())):
        total = total.astype(LOW)
        for z in range(2):
            for i in range(8):
                start = ((2 * part + z) * 8 + i) * own
                attn_ref[start : start + own, narrow:] = total[
                    z * own : (z + 1) * own, i * wide : (i + 1) * wide
                ]
    output_ref[:half] = (work[:half] + outs.upper_sum()).astype(LOW)
    output_ref[half:] = (work[half:] + outs.lower_sum()).astype(LOW)
    for c in done:
        c.wait()
    for c in swaps:
        c.wait_send()
    weights.sent()
    outs.sent()


def layer_turn(gh, mid, cot, gains, wo_all, part, tok, query, key, value, att, lengths, h1, columns):
    rows, width = mid.shape
    streams, length, wide = value.shape
    qk = query.shape[2]
    shape = jax.ShapeDtypeStruct
    f32 = jnp.float32
    anywhere = pl.BlockSpec(memory_space=pl.ANY)
    in_vmem = pl.BlockSpec(memory_space=pltpu.VMEM)
    dma = pltpu.SemaphoreType.DMA
    vmem = pltpu.VMEM
    arriving = [
        vmem((4, rows, width), LOW),
        vmem((4, rows // 2, width), LOW),
        vmem((2, rows // 2, width), LOW),
    ]
    return pl.pallas_call(
        turn_kernel,
        out_shape=[
            shape((rows, width), LOW),
            shape((rows, width), f32),
            shape((streams, length, columns), LOW),
            shape((8, width), f32),
            shape((width, columns + wide), LOW),
        ],
        in_specs=[anywhere] * 3
        + [in_vmem]
        + [anywhere] * 2
        + [in_vmem] * 5
        + [pl.BlockSpec(memory_space=pltpu.SMEM), anywhere],
        out_specs=[in_vmem, anywhere, anywhere, in_vmem, in_vmem],
        scratch_shapes=[
            vmem((rows, width), f32),
            vmem((rows, width), f32),
            vmem((rows, width), LOW),
            vmem((rows, width), LOW),
            vmem((streams, length, wide), LOW),
            vmem((streams, length, columns), LOW),
            vmem((2, width, wide), LOW),
            vmem((8, rows, width), LOW),
            vmem((4, rows, width), LOW),
            *arriving,
            *arriving,
            vmem((length, qk), f32),
            vmem((length, wide), f32),
            vmem((2, rows, width), LOW),
            vmem((width, columns), f32),
            dma((14,)),
            dma((14,)),
            dma((2, 10)),
            dma((2, 10)),
            dma((7,)),
            dma((2,)),
            dma((2,)),
            dma((2,)),
            dma((2,)),
        ],
        compiler_params=pltpu.CompilerParams(
            collective_id=22, has_side_effects=True, vmem_limit_bytes=63 * MIB
        ),
        cost_estimate=moved(16 * rows * width),
        name="turn",
    )(gh, mid, cot, gains, wo_all, part, tok, query, key, value, att, lengths, h1)


def close_kernel(
    g_ref,
    wa_ref,
    g_mid_ref,
    x_ref,
    gain_ref,
    sum_ref,
    blocks_ref,
    rest_ref,
    grad_ref,
    gains_ref,
    first_got,
    rest_got,
    beside,
    held,
    got,
    one,
    two,
    gain_rows,
    gain_line,
    gain_columns,
    gain_plane,
    blocks,
    first_sum,
    ssend,
    srecv,
    zsend,
    zrecv,
    esend,
    erecv,
    self_sem,
    fsend,
    frecv,
    f_sem,
):
    me, sib, xn, yn = partners()
    z = lax.axis_index("dp")
    rows, width = x_ref.shape
    span = rows // 2
    half = rows // 2
    f32 = jnp.float32
    barrier = pltpu.get_barrier_semaphore()
    for i in range(1, 8):
        pl.semaphore_signal(
            barrier, inc=1, device_id={"seq": lax.rem(me + i, 8)}, device_id_type=MESH
        )
    for i in range(1, 4):
        pl.semaphore_signal(
            barrier, inc=1, device_id={"dp": lax.rem(z + i, 4)}, device_id_type=MESH
        )
    pl.semaphore_wait(barrier, 10)
    load = pltpu.make_async_copy(blocks_ref, blocks, f_sem.at[0])
    load.start()
    keep = first_got.shape[1]

    def exchange(item, source, target):
        mine = pltpu.make_async_copy(
            source.at[pl.ds(me * keep, keep)], target.at[me], f_sem.at[1 + item]
        )
        mine.start()
        copies = []
        for i in range(1, 8):
            other = lax.rem(me + i, 8)
            copies.append(
                remote(
                    fsend,
                    frecv,
                    7 * item + i - 1,
                    source.at[pl.ds(other * keep, keep)],
                    target.at[me],
                    other,
                )
            )
            copies[-1].start()
        return mine, copies

    moves = [exchange(1, rest_ref, rest_got)]
    scatter = PlaneScatter(
        lambda i: beside.at[i], lambda i: held.at[i], got, one, two, ssend, srecv
    )
    def part_of(owner):
        there = pl.ds(pl.multiple_of(owner * span, span), span)
        grads = jnp.concatenate([g_ref[0, there, :], g_ref[1, there, :]], axis=0)
        return contract(grads, wa_ref[...], 1, 1).astype(LOW)

    owners = chips()
    for i in (2, 1, 3, 0):
        beside[i] = part_of(owners[i] + sib - me)
        scatter.start_pair(i)
        held[i] = part_of(owners[i])
        scatter.add_pair(i)

    load.wait()
    for second in range(2):
        total = jnp.zeros(blocks.shape[2:], f32)
        for owner in range(4):
            came = jnp.abs(z - owner) < 3
            total = total + jnp.where(came, blocks[owner, second].astype(f32), 0.0)
        lanes_here = total.shape[1]
        first_sum[:, second * lanes_here : (second + 1) * lanes_here] = total.astype(LOW)
    moves.append(exchange(0, first_sum, first_got))

    scatter.second()

    x = x_ref[...].astype(f32)
    inverse = norm_scale(x)
    normed = x * inverse
    gain = gain_ref[0:1, :].astype(f32)

    def finish(start, g_h):
        part = slice(start, start + half)
        grad_ref[part] = g_mid_ref[part] + norm_backward(g_h, normed[part], inverse[part], gain)
        return jnp.sum(g_h * normed[part], axis=0, keepdims=True)

    gain_sum = finish(0, scatter.upper_sum()) + finish(half, scatter.lower_sum())

    both = jnp.concatenate([gain_sum, sum_ref[0:1, :], jnp.zeros((14, width), f32)], axis=0)
    gain_rows[...] = both.astype(LOW)
    depth = width // 4

    def lanes(owner):
        return pl.ds(pl.multiple_of(owner * depth, 128), depth)

    def over_line(k, to, owner):
        return pltpu.make_async_remote_copy(
            src_ref=gain_rows.at[:, lanes(to)],
            dst_ref=gain_line.at[owner],
            send_sem=zsend.at[k],
            recv_sem=zrecv.at[owner],
            device_id={"dp": to},
            device_id_type=MESH,
        )

    others = [lax.rem(z + o, 4) for o in (1, 2, 3)]
    sends = [over_line(k, other, z) for k, other in enumerate(others)]
    own = pltpu.make_async_copy(gain_rows.at[:, lanes(z)], gain_line.at[z], self_sem.at[0])
    own.start()
    for c in sends:
        c.start()
    own.wait()
    for other in others:
        over_line(0, other, other).wait_recv()
    total = gain_line[0].astype(f32)
    for k in range(1, 4):
        total = total + gain_line[k].astype(f32)
    entry = lax.broadcasted_iota(jnp.int32, (16, 128), 0)
    lane = lax.broadcasted_iota(jnp.int32, (16, 128), 1)
    pick = jnp.where(lane == entry, 1.0, 0.0).astype(LOW)
    gain_columns[...] = contract(total.astype(LOW), pick, 0, 0).astype(LOW)
    count = depth // 8
    own = pltpu.make_async_copy(
        gain_columns.at[pl.ds(me * count, count)], gain_plane.at[me], self_sem.at[1]
    )
    own.start()
    swaps = []
    for i in range(1, 8):
        other = lax.rem(me + i, 8)
        swaps.append(
            remote(
                esend,
                erecv,
                i - 1,
                gain_columns.at[pl.ds(other * count, count)],
                gain_plane.at[me],
                other,
            )
        )
        swaps[-1].start()
    own.wait()
    for c in swaps:
        c.wait_recv()
    total = gain_plane[0].astype(f32)
    for k in range(1, 8):
        total = total + gain_plane[k].astype(f32)
    gains_ref[...] = total
    scatter.sent()
    for c in (*sends, *swaps):
        c.wait_send()
    for mine, copies in moves:
        mine.wait()
        for c in copies:
            c.wait()


def layer_close(g_all, wa, g_mid, tokens, gains, gain_sum, blocks, rest):
    rows, width = tokens.shape
    shape = jax.ShapeDtypeStruct
    in_vmem = pl.BlockSpec(memory_space=pltpu.VMEM)
    anywhere = pl.BlockSpec(memory_space=pl.ANY)
    dma = pltpu.SemaphoreType.DMA
    vmem = pltpu.VMEM
    return pl.pallas_call(
        close_kernel,
        out_shape=[
            shape((rows, width), jnp.float32),
            shape((width // 32, 128), jnp.float32),
            shape((8, width // 32, 8 * CHUNKS[0]), LOW),
            shape((8, width // 32, rest.shape[1]), LOW),
        ],
        in_specs=[in_vmem] * 6 + [anywhere] * 2,
        out_specs=[in_vmem, in_vmem, anywhere, anywhere],
        scratch_shapes=[
            vmem((4, rows, width), LOW),
            vmem((4, rows, width), LOW),
            vmem((4, rows, width), LOW),
            vmem((4, rows // 2, width), LOW),
            vmem((2, rows // 2, width), LOW),
            vmem((16, width), LOW),
            vmem((4, 16, width // 4), LOW),
            vmem((width // 4, 128), LOW),
            vmem((8, width // 32, 128), LOW),
            vmem(blocks.shape, LOW),
            vmem((width // 4, 8 * CHUNKS[0]), LOW),
            dma((10,)),
            dma((10,)),
            dma((3,)),
            dma((4,)),
            dma((7,)),
            dma((7,)),
            dma((2,)),
            dma((14,)),
            dma((14,)),
            dma((3,)),
        ],
        compiler_params=pltpu.CompilerParams(
            collective_id=23, has_side_effects=True, vmem_limit_bytes=56 * MIB
        ),
        cost_estimate=moved(16 * rows * width),
        name="close",
    )(g_all, wa, g_mid, tokens, gains, gain_sum, blocks, rest)


def place_kernel(
    first_ref,
    rest_ref,
    blocks_ref,
    down_ref,
    out_ref,
    grad_ref,
    gate_out,
    up_out,
    down_out,
    out_copy,
    grad_copy,
    sems,
):
    copies = [
        pltpu.make_async_copy(out_ref, out_copy, sems.at[0]),
        pltpu.make_async_copy(grad_ref, grad_copy, sems.at[1]),
    ]
    for c in copies:
        c.start()
    f32 = jnp.float32
    z = lax.axis_index("dp")
    share = sum(CHUNKS)
    for second, target in enumerate((gate_out, up_out)):
        for owner in range(8):
            for group in range(4):
                at = group * 8 * share + owner * share
                start = 0
                for k, count in enumerate(CHUNKS):
                    source = first_ref if k == 0 else rest_ref
                    begin = start + (4 * second + group) * count
                    target[:, at : at + count] = source[owner, :, begin : begin + count].astype(f32)
                    at += count
                    start += 8 * count if k else 0
    total = jnp.zeros(blocks_ref.shape[1:], f32)
    for owner in range(4):
        came = jnp.abs(z - owner) < 3
        total = total + jnp.where(came, blocks_ref[owner].astype(f32), 0.0)
    down_out[: CHUNKS[0], :] = total
    down_out[CHUNKS[0] :, :] = down_ref[...].astype(f32)
    for c in copies:
        c.wait()


def place_rows(first, rest, blocks, down, output, input_grad):
    own, width = first.shape[1], blocks.shape[2]
    shape = jax.ShapeDtypeStruct
    anywhere = pl.BlockSpec(memory_space=pl.ANY)
    in_vmem = pl.BlockSpec(memory_space=pltpu.VMEM)
    wide = 32 * sum(CHUNKS)
    return pl.pallas_call(
        place_kernel,
        out_shape=[
            shape((own, wide), jnp.float32),
            shape((own, wide), jnp.float32),
            shape((sum(CHUNKS), width), jnp.float32),
            shape(output.shape, output.dtype),
            shape(input_grad.shape, input_grad.dtype),
        ],
        in_specs=[in_vmem] * 4 + [anywhere] * 2,
        out_specs=[in_vmem] * 3 + [anywhere] * 2,
        scratch_shapes=[pltpu.SemaphoreType.DMA((2,))],
        compiler_params=pltpu.CompilerParams(vmem_limit_bytes=40 * MIB),
        name="place",
    )(first, rest, blocks, down, output, input_grad)


def place_attn_kernel(got_ref, out_ref, query_out, key_out, value_out, grad_out):
    f32 = jnp.float32
    wide = value_out.shape[1] // 8
    qk = query_out.shape[1] // 8
    own = out_ref.shape[0] // 8
    for owner in range(8):
        value_out[:, owner * wide : (owner + 1) * wide] = got_ref[owner, :, :wide].astype(f32)
        here = slice(owner * qk, (owner + 1) * qk)
        query_out[:, here] = got_ref[owner, :, wide : wide + qk].astype(f32)
        key_out[:, here] = got_ref[owner, :, wide + qk : wide + 2 * qk].astype(f32)
        block = out_ref[owner * own : (owner + 1) * own, out_ref.shape[1] - wide :]
        grad_out[:, owner * wide : (owner + 1) * wide] = block.astype(f32)


def place_attn(got, summed, wide, qk):
    own = got.shape[1]
    shape = jax.ShapeDtypeStruct
    in_vmem = pl.BlockSpec(memory_space=pltpu.VMEM)
    return pl.pallas_call(
        place_attn_kernel,
        out_shape=[
            shape((own, 8 * qk), jnp.float32),
            shape((own, 8 * qk), jnp.float32),
            shape((own, 8 * wide), jnp.float32),
            shape((own, 8 * wide), jnp.float32),
        ],
        in_specs=[in_vmem] * 2,
        out_specs=[in_vmem] * 4,
        name="place_attn",
    )(got, summed)


def ffn_lax(h_two, cot_all, gate_full, up_full, down_full):
    pieces, rows, width = cot_all.shape
    h_two_all = gather_plane(h_two, 5).reshape(-1, width)
    cot_all = cot_all.reshape(-1, width)
    gate = dot(h_two_all, gate_full)
    up = dot(h_two_all, up_full)
    g_act = contract(cot_all, down_full, 1, 1)
    sigmoid = jax.nn.sigmoid(gate)
    silu = gate * sigmoid
    act = (silu * up).astype(LOW)
    g_gate = (g_act * up * sigmoid * (1.0 + gate * (1.0 - sigmoid))).astype(LOW)
    g_up = (g_act * silu).astype(LOW)
    part = (contract(g_gate, gate_full, 1, 1) + contract(g_up, up_full, 1, 1)).astype(LOW)
    return (
        dot(act, down_full).astype(LOW).reshape(pieces, rows, width),
        scatter_plane(part.reshape(pieces, rows, width), 7),
        contract(h_two_all, g_gate, 0, 0).astype(LOW),
        contract(h_two_all, g_up, 0, 0).astype(LOW),
        contract(act, cot_all, 0, 0).astype(LOW),
    )


def norm_scale(rows):
    return lax.rsqrt(jnp.mean(rows * rows, axis=-1, keepdims=True) + epsilon)


def norm_backward(grad, normed, inverse, gain):
    scaled = grad * gain
    return inverse * (scaled - normed * jnp.mean(scaled * normed, axis=-1, keepdims=True))


def local(
    tokens,
    doc_lengths,
    w_query,
    w_key,
    w_value,
    w_out,
    w_gate,
    w_up,
    w_down,
    gain_attn,
    gain_mlp,
    cotangent,
):
    micro, span = tokens.shape[1:3]
    pieces, groups = lax.axis_size("seq"), lax.axis_size("dp")
    place = lax.axis_index("seq")
    length = pieces * span
    heads = max(1, HEADS // pieces)
    sharers = max(1, pieces // HEADS)
    streams = micro // sharers
    first_head = place // sharers * heads
    first_stream = place % sharers * streams
    qk, wide = heads * QK_DIM, heads * HEAD_V
    hidden = FF // pieces

    out_width = D // pieces
    rows_dp = w_gate.shape[0]
    share = hidden // groups
    block = FF // groups
    mine = micro * span
    fused = pieces == 8 and groups == 4 and micro == 2 and span == 128
    chunks = CHUNKS if fused else (share,)

    def hidden_columns(w):
        parts = [
            lax.dynamic_slice_in_dim(w, z * block + place * share, share, 1) for z in range(groups)
        ]
        edges = [sum(chunks[:k]) for k in range(len(chunks) + 1)]
        return [
            [part[:, edges[k] : edges[k + 1]] for part in parts] for k in range(len(chunks))
        ]

    x_own = tokens[0].reshape(mine, D)
    flat = x_own.astype(jnp.float32)
    cot = cotangent[0].reshape(mine, D)

    def to_tokens(by_head):
        sent = by_head.reshape(streams, pieces, span, wide).transpose(1, 0, 2, 3)
        got = exchange_plane(sent, 3).reshape(pieces // sharers, micro, span, wide)
        return got.transpose(1, 2, 0, 3).reshape(mine, HEADS * HEAD_V)

    def to_heads(by_token):
        sent = by_token.reshape(micro, span, pieces // sharers, wide).transpose(2, 0, 1, 3)
        got = exchange_plane(sent.reshape(pieces, streams, span, wide), 4)
        return got.transpose(1, 0, 2, 3).reshape(streams, length, wide)

    if fused:
        gain_rows = jnp.concatenate(
            [gain_attn[None], gain_mlp[None], jnp.zeros((14, rows_dp), LOW)], axis=0
        )
        weights = (w_query, w_key, w_value, w_out, w_gate, w_up, w_down)
        front = layer_front(x_own, cot, weights, gain_rows, doc_lengths[0], length, wide, qk)
        out_full, h_all, query, key, value, att_heads, attended, mid = front[3:11]
        attn_full, gain_rows_all, out_part, g_h_two = front[11:15]
        d_ffn, d_down, ffn_blocks, down_blocks = front[17:]
    else:
        gate_parts, up_parts = hidden_columns(w_gate), hidden_columns(w_up)
        ffn_slice = jnp.concatenate(
            [part for k in range(len(chunks)) for part in gate_parts[k] + up_parts[k]], axis=1
        )
        attn_parts = [
            lax.dynamic_slice_in_dim(w_value, first_head * HEAD_V, wide, 1),
            lax.dynamic_slice_in_dim(w_query, first_head * QK_DIM, qk, 1),
            lax.dynamic_slice_in_dim(w_key, first_head * QK_DIM, qk, 1),
        ]

        lengths = lax.dynamic_slice_in_dim(doc_lengths[0], first_stream, streams, 0)
        starts = jnp.cumsum(lengths, axis=1) - lengths
        position = jnp.arange(length, dtype=jnp.int32)
        begun = starts[:, None, :] <= position[None, :, None]
        first = jnp.max(jnp.where(begun, starts[:, None, :], 0), axis=2)[..., None]

        def gather_dp(w):
            return lax.all_gather(w, "dp", axis=0, tiled=True)

        attn_got = gather_dp(
            jnp.concatenate(
                attn_parts
                + [
                    lax.dynamic_slice_in_dim(w_out, place * out_width, out_width, 1),
                    gain_attn[:, None],
                    gain_mlp[:, None],
                ],
                axis=1,
            )
        )
        ffn_full = gather_dp(ffn_slice)
        down_full = gather_dp(lax.dynamic_slice_in_dim(w_down, place * share, share, 0))
        value_full = attn_got[:, :wide]
        query_full = attn_got[:, wide : wide + qk]
        key_full = attn_got[:, wide + qk : wide + 2 * qk]
        out_full = gather_plane(attn_got[:, wide + 2 * qk : wide + 2 * qk + out_width], 2)
        gains = attn_got[:, wide + 2 * qk + out_width :].astype(jnp.float32)
        gain_one, gain_two = gains[:, 0], gains[:, 1]
        x_all = gather_plane(x_own, 1).reshape(pieces, micro, span, D).transpose(1, 0, 2, 3)
        x_all = lax.dynamic_slice_in_dim(x_all, first_stream, streams, 0).astype(jnp.float32)
        h_flat = (x_all * norm_scale(x_all) * gain_one).astype(LOW).reshape(streams * length, D)
        value = dot(h_flat, value_full).astype(LOW).reshape(streams, length, wide)
        query = dot(h_flat, query_full).astype(LOW).reshape(streams, length, qk)
        key = dot(h_flat, key_full).astype(LOW).reshape(streams, length, qk)
        att_heads = attend(query, key, value, first, heads)
        attended = to_tokens(att_heads)
        mid = flat + jnp.einsum(
            "tk,skn->tsn", attended, out_full, preferred_element_type=jnp.float32
        ).reshape(mine, D)
        h_two = (mid * norm_scale(mid) * gain_two).astype(LOW)
        out_part, g_h_two, d_gate, d_up, d_down = ffn_lax(
            h_two, gather_plane(cot, 6), ffn_full[:, :hidden], ffn_full[:, hidden:], down_full
        )
        d_ffn = jnp.concatenate([d_gate, d_up], axis=1)

    def scatter_dp(part):
        return lax.psum_scatter(part, "dp", scatter_dimension=0, tiled=True)

    own = rows_dp // pieces
    sum_ffn, sum_down = scatter_dp(d_ffn), scatter_dp(d_down)

    if fused:
        output, g_mid, g_all, gain_sum, grad_attn = layer_turn(
            g_h_two, mid, cot, gain_rows_all, out_full, out_part, attended, query, key, value,
            att_heads, doc_lengths[0], h_all, attn_full.shape[1],
        )
        grad_attn, sum_ffn, sum_down = lax.optimization_barrier((grad_attn, sum_ffn, sum_down))
        grad_attn = scatter_dp(grad_attn)
        input_grad, gain_columns, first_got, rest_got = layer_close(
            g_all, attn_full, g_mid, x_own, gain_rows_all, gain_sum, ffn_blocks, sum_ffn
        )
        grad_gate, grad_up, grad_down, output, input_grad = place_rows(
            first_got, rest_got, down_blocks, sum_down, output, input_grad
        )
        grad_attn, grad_gate = lax.optimization_barrier((grad_attn, grad_gate))
        attn_got = exchange_plane(grad_attn[:, : attn_full.shape[1]].reshape(pieces, own, -1), 12)
        grad_query, grad_key, grad_value, grad_out = place_attn(attn_got, grad_attn, wide, qk)
        return (
            output.reshape(tokens.shape),
            input_grad.reshape(tokens.shape),
            grad_query,
            grad_key,
            grad_value,
            grad_out,
            grad_gate,
            grad_up,
            grad_down,
            gain_columns[:, 0],
            gain_columns[:, 1],
        )

    inverse_two = norm_scale(mid)
    plain_two = mid * inverse_two
    output = (mid + scatter_plane(out_part, 8)).astype(LOW)
    g_mid = cot.astype(jnp.float32) + norm_backward(g_h_two, plain_two, inverse_two, gain_two)
    g_mid_low = g_mid.astype(LOW)
    g_att = jnp.einsum(
        "tsn,skn->tk",
        g_mid_low.reshape(mine, pieces, out_width),
        out_full,
        preferred_element_type=jnp.float32,
    )
    g_att = to_heads(g_att.astype(LOW))
    g_query, g_key, g_value = attend_back(query, key, value, first, att_heads, g_att, heads)
    g_value = g_value.reshape(streams * length, wide)
    g_query = g_query.reshape(streams * length, qk)
    g_key = g_key.reshape(streams * length, qk)
    g_h_one_part = (
        contract(g_value, value_full, 1, 1)
        + contract(g_query, query_full, 1, 1)
        + contract(g_key, key_full, 1, 1)
    ).astype(LOW)
    g_h_one_part = g_h_one_part.reshape(streams, pieces, span, D).transpose(1, 0, 2, 3)
    if sharers > 1:
        padded = jnp.zeros((pieces, micro, span, D), LOW)
        g_h_one_part = lax.dynamic_update_slice_in_dim(padded, g_h_one_part, first_stream, 1)
    g_h_one = scatter_plane(g_h_one_part.reshape(pieces, mine, D), 9)
    inverse_one = norm_scale(flat)
    plain_one = flat * inverse_one
    input_grad = g_mid + norm_backward(g_h_one, plain_one, inverse_one, gain_one)
    grad_out = contract(attended, g_mid_low, 0, 0).astype(LOW)
    grad_out = grad_out.reshape(groups, pieces, own, D).transpose(1, 0, 2, 3)
    grad_out = scatter_plane(grad_out.reshape(pieces, groups * own, D), 10).astype(LOW)
    grad_out = scatter_dp(grad_out)
    grad_attn = jnp.concatenate(
        [
            contract(h_flat, g_value, 0, 0).astype(LOW),
            contract(h_flat, g_query, 0, 0).astype(LOW),
            contract(h_flat, g_key, 0, 0).astype(LOW),
            jnp.sum(g_h_one * plain_one, axis=0).astype(LOW)[:, None],
            jnp.sum(g_h_two * plain_two, axis=0).astype(LOW)[:, None],
        ],
        axis=1,
    )

    grad_attn = scatter_dp(grad_attn)
    ffn_got = exchange_plane(sum_ffn.reshape(pieces, own, 2 * hidden), 11).astype(jnp.float32)
    attn_got = exchange_plane(grad_attn.reshape(pieces, own, -1), 12).astype(jnp.float32)
    grad_gains = jnp.sum(attn_got[:, :, wide + 2 * qk :], axis=0)
    attn_got = jnp.sum(attn_got.reshape(pieces // sharers, sharers, own, -1), axis=1)

    def by_hidden(block):
        return block.reshape(pieces, own, groups, share).transpose(1, 2, 0, 3).reshape(own, FF)

    def by_rows(block):
        return block.transpose(1, 0, 2).reshape(own, -1)

    return (
        output.reshape(tokens.shape),
        input_grad.reshape(tokens.shape),
        by_rows(attn_got[:, :, wide : wide + qk]),
        by_rows(attn_got[:, :, wide + qk : wide + 2 * qk]),
        by_rows(attn_got[:, :, :wide]),
        grad_out.astype(jnp.float32),
        by_hidden(ffn_got[:, :, :hidden]),
        by_hidden(ffn_got[:, :, hidden:]),
        sum_down.astype(jnp.float32),
        grad_gains[:, 0],
        grad_gains[:, 1],
    )


def solution(mesh):
    by_token, by_row = P("dp", None, "seq", None), P("dp", None)
    grad_rows, grad_entries = P(("dp", "seq"), None), P(("dp", "seq"))
    return jax.shard_map(
        local,
        mesh=mesh,
        in_specs=(by_token, P("dp", None, None)) + (by_row,) * 7 + (P("dp"), P("dp"), by_token),
        out_specs=(by_token, by_token) + (grad_rows,) * 7 + (grad_entries,) * 2,
        check_vma=False,
    )
```

profile of v0, /device:TPU:1, one launch (start us, length us, event | category | flops | bytes accessed | tf_op | source)
XLA Modules:
  0.0 499.6 jit_solution(14004222691831799512)
XLA Ops:
  7.2 0.0 reduce-scatter.6.cloned.1.call-start
  7.2 0.7 broadcast_in_dim.9
  7.9 0.7 broadcast_in_dim.10
  8.6 0.1 pad.2.clone
  8.7 0.7 maximum_maximum_fusion.gain_ref
  9.4 285.4 %layer.1 = (bf16[8,256,2048]{2,1,0:T(8,128)(2,1)}, bf16[8,256,2048]{2,1,0:T(8,128)(2,1)}, bf16[8,256,2048]{2,1,0:T(8,128)(2,1)}, bf16[8,2048,256]{2,1,0:T(8,128)...) custom-call(bf16[256,2048]{1,0:T(8,128)(2,1)} %bitcast.9, ...), custom_call_target="tpu_custom_call" | custom-call | flops 53150220288 | bytes 209715200 | tf_op jit(solution)/shard_map/layer/pallas_call | solution.py:1343
  294.8 0.0 reduce-scatter.6.cloned.1.call-update
  294.8 0.0 reduce-scatter.4.cloned.1.call-start
  294.8 0.7 reduce-scatter.4.cloned.1.call-update
  295.5 0.0 reduce-scatter.8.cloned.1.call-start
  295.6 103.2 %turn.1 = (bf16[256,2048]{1,0:T(8,128)(2,1)}, f32[256,2048]{1,0:T(8,128)}, bf16[2,1024,384]{2,1,0:T(8,128)(2,1)}, f32[8,2048]{1,0:T(8,128)}, bf16[2048,640]{1,0:T(8,128)(2,1)}) custom-call(f32[256,2048]{1,0:T(8,128)} %get-tuple-element.50.gh_ref, f32[256,2048]{1,0:T(8,128)} %get-tuple-element.51.mid_ref, bf16[256,2048]{1,0:T(8,128)(2,1)} %bitcast.8, ...), custom_call_target="tpu_custom_call" | custom-call | bytes 83886080 | tf_op jit(solution)/shard_map/turn/pallas_call | solution.py:1848
  398.8 0.0 reduce-scatter.6.cloned.1.call-done.down_ref
  398.9 3.5 reduce-scatter.4.cloned.1.call-done.rest_ref
  402.3 0.0 reduce-scatter.8.cloned.1.call-update
  402.3 0.0 copy-start.1
  402.4 0.0 copy-start.2
  402.4 0.0 copy-start.5
  402.4 68.9 %close.1 = (f32[256,2048]{1,0:T(8,128)}, f32[64,128]{1,0:T(8,128)}, bf16[8,64,512]{2,1,0:T(8,128)(2,1)}, bf16[8,64,896]{2,1,0:T(8,128)(2,1)}) custom-call(bf16[2,1024,384]{2,1,0:T(8,128)(2,1)} %get-tuple-element.61.g_ref, bf16[2048,384]{1,0:T(8,128)(2,1)} %get-tuple-element.62.wa_ref, f32[256,2048]{1,0:T(8,128)} %get-tuple-element.63.g_mid_ref, ...), custom_call_target="tpu_custom_call" | custom-call | bytes 83886080 | tf_op jit(solution)/shard_map/close/pallas_call | solution.py:2088
  471.3 0.0 copy-done.1
  471.3 0.0 copy-done.2
  471.3 0.0 copy-done.5
  471.3 0.0 copy-start
  471.3 1.6 copy-done
  472.9 0.0 copy-start.3
  472.9 1.2 copy-done.3
  474.1 0.0 copy-start.4
  474.1 1.0 copy-done.4
  475.1 0.0 copy-start.6
  475.1 4.6 place.1
  479.7 0.0 copy-done.6
  479.7 0.7 slice_reduce_fusion
  480.4 0.0 reduce-scatter.8.cloned.1.call-done.out_ref
  480.4 1.8 slice.9
  482.2 8.3 %exchange.1.got_ref = bf16[8,64,384]{2,1,0:T(8,128)(2,1)} custom-call(bf16[8,64,384]{2,1,0:T(8,128)(2,1)} %bitcast.6), custom_call_target="tpu_custom_call" | custom-call | bytes 7864320 | tf_op jit(solution)/shard_map/exchange/pallas_call | solution.py:341
  490.5 2.3 place_attn.1
  (1 shorter events, 0.0 us)
Async XLA Ops:
  7.2 391.7 %reduce-scatter.6.cloned.1.call-start = ((), (), s32[]{:S(2)}) async-start(), calls=%async_computation.4 | async-start | bytes 2293760 | tf_op jit(solution)/shard_map/reduce_scatter | solution.py:2382
  294.8 107.5 %reduce-scatter.4.cloned.1.call-start = ((), (), s32[]{:S(2)}) async-start(), calls=%async_computation.3 | async-start | bytes 4587520 | tf_op jit(solution)/shard_map/reduce_scatter | solution.py:2382
  295.5 184.8 %reduce-scatter.8.cloned.1.call-start = ((), (), s32[]{:S(2)}) async-start(), calls=%async_computation.5 | async-start | bytes 3276800 | tf_op jit(solution)/shard_map/reduce_scatter | solution.py:2382
  402.3 68.9 %copy-start.1 = (bf16[4,64,2048]{2,1,0:T(8,128)(2,1)S(1)}, bf16[4,64,2048]{2,1,0:T(8,128)(2,1)}, u32[]{:S(2)}) copy-start(bf16[4,64,2048]{2,1,0:T(8,128)(2,1)} %get-tuple-element.72.blocks_ref) | copy-start | bytes 3145732
  402.4 68.9 %copy-start.2 = (bf16[256,2048]{1,0:T(8,128)(2,1)S(1)}, bf16[256,2048]{1,0:T(8,128)(2,1)}, u32[]{:S(2)}) copy-start(bf16[256,2048]{1,0:T(8,128)(2,1)} %get-tuple-element.74.out_ref) | copy-start | bytes 3145732
  402.4 68.9 %copy-start.5 = (bf16[112,2048]{1,0:T(8,128)(2,1)S(1)}, bf16[112,2048]{1,0:T(8,128)(2,1)}, u32[]{:S(2)}) copy-start(bf16[112,2048]{1,0:T(8,128)(2,1)} %reduce-scatter.6.cloned.1.call-done.down_ref) | copy-start | bytes 1376260
  471.3 1.6 copy-start
  472.9 1.2 copy-start.3
  474.1 1.0 copy-start.4
  475.1 4.6 copy-start.6
Sparse Core Ops, SparseCore 0:
  294.9 37.4 reduce-scatter.5
  334.7 67.5 reduce-scatter.3
  404.6 52.4 reduce-scatter.7
where the time goes:
time: 505 us; the launch traced here: 500 us
  Pallas kernels  473 us (94%)
  between operations  14.1 us (3%)
  local copies, waits for them, and re-layouts  7.75 us (2%)
    pallas_call x1, Pallas kernels, layer_front(): pl.pallas_call(layer_kernel, out_shape=out_shape, in_specs=[anywhere] * 1...  285 us
    pallas_call x1, Pallas kernels, layer_turn(): pl.pallas_call(turn_kernel, out_shape=[shape((rows, width), LOW), shape((...  103 us
    pallas_call x1, Pallas kernels, layer_close(): pl.pallas_call(close_kernel, out_shape=[shape((rows, width), jnp.float32)...  68.9 us
  transfers between devices with their start and end apart: 3, of which 1 were waited for; matrix products, arithmetic and copies ran while one was open for 0% of the time, Pallas kernels for 35%

commit v1 on v0

--- a/solution.py
+++ b/solution.py
@@ -320,12 +320,13 @@
 
 def exchange_kernel(x_ref, o_ref, send, recv, own_sem):
     me = lax.axis_index("seq")
+    columns = pl.ds(0, o_ref.shape[2])
     others = [lax.rem(me + i, 8) for i in range(1, 8)]
     greet(others)
-    own = pltpu.make_async_copy(x_ref.at[me], o_ref.at[me], own_sem)
+    own = pltpu.make_async_copy(x_ref.at[me, :, columns], o_ref.at[me], own_sem)
     own.start()
     copies = [
-        remote(send, recv, i, x_ref.at[other], o_ref.at[me], other)
+        remote(send, recv, i, x_ref.at[other, :, columns], o_ref.at[me], other)
         for i, other in enumerate(others)
     ]
     for c in copies:
@@ -335,12 +336,12 @@
         c.wait()
 
 
-def exchange_plane(x, number):
+def exchange_plane(x, number, columns=None):
     if lax.axis_size("seq") != 8:
         return lax.all_to_all(x, "seq", 0, 0)
     return pl.pallas_call(
         exchange_kernel,
-        out_shape=jax.ShapeDtypeStruct(x.shape, x.dtype),
+        out_shape=jax.ShapeDtypeStruct(x.shape[:-1] + (columns or x.shape[-1],), x.dtype),
         in_specs=[pl.BlockSpec(memory_space=pl.ANY)],
         out_specs=pl.BlockSpec(memory_space=pl.ANY),
         scratch_shapes=[
@@ -747,6 +748,9 @@
             at = columns[k] + (4 * second + group) * count
             wgu[there, at : at + count] = rolled[:, begin : begin + count].astype(LOW)
             begin += count
+    z_out.start()
+    for g in (z_up[0], z_down[0]):
+        g.start()
 
     def loads(order, step, sources):
         slot = lax.rem(step, 2)
@@ -758,16 +762,20 @@
 
     first_load = pltpu.make_async_copy(x_ref, x_buf.at[0], load_sem.at[0, 0])
     first_load.start()
-    own_c = pltpu.make_async_copy(c_ref, c_all.at[me], self_sem.at[3])
-    own_c.start()
+    c_load = pltpu.make_async_copy(c_ref, c_buf.at[0], load_sem.at[1, 0])
+    c_load.start()
     tokens.forward_first()
     z_gain.forward()
     z_attn.forward()
     tokens.forward_second()
     cots.start()
+    c_load.wait()
+    own_c = pltpu.make_async_copy(c_buf.at[0], c_all.at[me], self_sem.at[3])
+    own_c.start()
     z_gain.wait()
     z_attn.wait()
-    z_out.start()
+    for g in (z_up[1], z_down[1]):
+        g.start()
 
     def h1_copies(step):
         slot = lax.rem(step, 2)
@@ -795,11 +803,6 @@
             tokens.forward_third()
             tokens.from_sibling("y")
 
-        @pl.when(step == 3)
-        def _():
-            for g in (z_up[0], z_down[0]):
-                g.start()
-
         @pl.when(step == 6)
         def _():
             tokens.from_sibling("diag")
@@ -849,7 +852,7 @@
             c.wait()
     z_out.wait()
     out_w.start()
-    for g in (z_up[1], z_down[1]):
+    for g in (z_up[2], z_down[2]):
         g.start()
 
     finals = [
@@ -936,8 +939,6 @@
     cots.forward_second()
     z_up[0].forward()
     z_down[0].forward()
-    for g in (z_up[2], z_down[2]):
-        g.start_far()
     for c in kept:
         c.wait()
     for c in swaps:
@@ -984,9 +985,9 @@
     hidden_in.start()
     own_h2 = pltpu.make_async_copy(held.at[0], h2_all.at[me], self_sem.at[2])
     own_h2.start()
-    for g in (z_up[2], z_down[2]):
-        g.start_near()
     cots.forward_third()
+    z_up[1].forward()
+    z_down[1].forward()
     own_h2.wait()
     own_c.wait()
     z_up[0].wait()
@@ -1123,11 +1124,6 @@
         def _():
             cots.from_sibling("diag")
 
-        @pl.when(step == 7)
-        def _():
-            z_up[2].forward()
-            z_down[2].forward()
-
     for c in loads(nearest_first, 0, sources):
         c.start()
 
@@ -1139,11 +1135,11 @@
     lax.fori_loop(0, 4, functools.partial(forward_pass, (0,), 3, arrive_near), 0)
     for c in loads(nearest_first, 0, sources):
         c.start()
-    z_up[1].forward()
-    z_down[1].forward()
     z_up[1].wait()
     z_down[1].wait()
     lax.fori_loop(0, 4, functools.partial(forward_pass, (1,), 3, None), 0)
+    z_up[2].forward()
+    z_down[2].forward()
     arrive_both(jnp.int32(4))
     for c in loads(nearest_first, 4, sources):
         c.start()
@@ -2127,10 +2123,10 @@
 
 
 def place_kernel(
-    first_ref,
-    rest_ref,
-    blocks_ref,
-    down_ref,
+    first_in,
+    rest_in,
+    blocks_in,
+    down_in,
     out_ref,
     grad_ref,
     gate_out,
@@ -2138,14 +2134,29 @@
     down_out,
     out_copy,
     grad_copy,
+    first_ref,
+    rest_ref,
+    blocks_ref,
+    down_ref,
     sems,
 ):
     copies = [
-        pltpu.make_async_copy(out_ref, out_copy, sems.at[0]),
-        pltpu.make_async_copy(grad_ref, grad_copy, sems.at[1]),
+        pltpu.make_async_copy(source, target, sems.at[i])
+        for i, (source, target) in enumerate(
+            (
+                (first_in, first_ref),
+                (rest_in, rest_ref),
+                (blocks_in, blocks_ref),
+                (down_in, down_ref),
+                (out_ref, out_copy),
+                (grad_ref, grad_copy),
+            )
+        )
     ]
     for c in copies:
         c.start()
+    for c in copies[:2]:
+        c.wait()
     f32 = jnp.float32
     z = lax.axis_index("dp")
     share = sum(CHUNKS)
@@ -2160,13 +2171,15 @@
                     target[:, at : at + count] = source[owner, :, begin : begin + count].astype(f32)
                     at += count
                     start += 8 * count if k else 0
+    for c in copies[2:4]:
+        c.wait()
     total = jnp.zeros(blocks_ref.shape[1:], f32)
     for owner in range(4):
         came = jnp.abs(z - owner) < 3
         total = total + jnp.where(came, blocks_ref[owner].astype(f32), 0.0)
     down_out[: CHUNKS[0], :] = total
     down_out[CHUNKS[0] :, :] = down_ref[...].astype(f32)
-    for c in copies:
+    for c in copies[4:]:
         c.wait()
 
 
@@ -2185,10 +2198,16 @@
             shape(output.shape, output.dtype),
             shape(input_grad.shape, input_grad.dtype),
         ],
-        in_specs=[in_vmem] * 4 + [anywhere] * 2,
-        out_specs=[in_vmem] * 3 + [anywhere] * 2,
-        scratch_shapes=[pltpu.SemaphoreType.DMA((2,))],
-        compiler_params=pltpu.CompilerParams(vmem_limit_bytes=40 * MIB),
+        in_specs=[anywhere] * 6,
+        out_specs=[in_vmem] * 5,
+        scratch_shapes=[
+            pltpu.VMEM(first.shape, LOW),
+            pltpu.VMEM(rest.shape, LOW),
+            pltpu.VMEM(blocks.shape, LOW),
+            pltpu.VMEM(down.shape, LOW),
+            pltpu.SemaphoreType.DMA((6,)),
+        ],
+        compiler_params=pltpu.CompilerParams(vmem_limit_bytes=63 * MIB),
         name="place",
     )(first, rest, blocks, down, output, input_grad)
 
@@ -2394,11 +2413,13 @@
         input_grad, gain_columns, first_got, rest_got = layer_close(
             g_all, attn_full, g_mid, x_own, gain_rows_all, gain_sum, ffn_blocks, sum_ffn
         )
+        grad_attn, gain_columns = lax.optimization_barrier((grad_attn, gain_columns))
+        kept = attn_full.shape[1]
+        attn_got = exchange_plane(grad_attn.reshape(pieces, own, -1), 12, kept)
+        attn_got, first_got = lax.optimization_barrier((attn_got, first_got))
         grad_gate, grad_up, grad_down, output, input_grad = place_rows(
             first_got, rest_got, down_blocks, sum_down, output, input_grad
         )
-        grad_attn, grad_gate = lax.optimization_barrier((grad_attn, grad_gate))
-        attn_got = exchange_plane(grad_attn[:, : attn_full.shape[1]].reshape(pieces, own, -1), 12)
         grad_query, grad_key, grad_value, grad_out = place_attn(attn_got, grad_attn, wide, qk)
         return (
             output.reshape(tokens.shape),

time: 505 us -> 500 us (0.990)
  no operation moved by 1% of the time
where the time goes in v1:
time: 500 us; the launch traced here: 495 us
  Pallas kernels  473 us (95%)
  between operations  14.1 us (3%)
    pallas_call x1, Pallas kernels, layer_front(): pl.pallas_call(layer_kernel, out_shape=out_shape, in_specs=[anywhere] * 1...  284 us
    pallas_call x1, Pallas kernels, layer_turn(): pl.pallas_call(turn_kernel, out_shape=[shape((rows, width), LOW), shape((...  104 us
    pallas_call x1, Pallas kernels, layer_close(): pl.pallas_call(close_kernel, out_shape=[shape((rows, width), jnp.float32)...  68.8 us
  transfers between devices with their start and end apart: 3, of which 1 were waited for; matrix products, arithmetic and copies ran while one was open for 0% of the time, Pallas kernels for 35%

profile of v1, /device:TPU:1, one launch (start us, length us, event | category | flops | bytes accessed | tf_op | source)
XLA Modules:
  0.0 495.2 jit_solution(15104651552588236374)
XLA Ops:
  7.2 0.0 reduce-scatter.6.cloned.1.call-start
  7.2 0.7 broadcast_in_dim.9
  7.9 0.7 broadcast_in_dim.10
  8.6 0.1 pad.2.clone
  8.7 0.7 maximum_maximum_fusion.gain_ref
  9.4 283.7 %layer.1 = (bf16[8,256,2048]{2,1,0:T(8,128)(2,1)}, bf16[8,256,2048]{2,1,0:T(8,128)(2,1)}, bf16[8,256,2048]{2,1,0:T(8,128)(2,1)}, bf16[8,2048,256]{2,1,0:T(8,128)...) custom-call(bf16[256,2048]{1,0:T(8,128)(2,1)} %bitcast.9, ...), custom_call_target="tpu_custom_call" | custom-call | flops 53150220288 | bytes 209715200 | tf_op jit(solution)/shard_map/layer/pallas_call | solution.py:1339
  293.1 0.0 reduce-scatter.6.cloned.1.call-update
  293.1 0.0 reduce-scatter.4.cloned.1.call-start
  293.1 0.7 reduce-scatter.4.cloned.1.call-update
  293.8 0.0 reduce-scatter.8.cloned.1.call-start
  293.9 103.8 %turn.1 = (bf16[256,2048]{1,0:T(8,128)(2,1)}, f32[256,2048]{1,0:T(8,128)}, bf16[2,1024,384]{2,1,0:T(8,128)(2,1)}, f32[8,2048]{1,0:T(8,128)}, bf16[2048,640]{1,0:T(8,128)(2,1)}) custom-call(f32[256,2048]{1,0:T(8,128)} %get-tuple-element.52.gh_ref, f32[256,2048]{1,0:T(8,128)} %get-tuple-element.53.mid_ref, bf16[256,2048]{1,0:T(8,128)(2,1)} %bitcast.8, ...), custom_call_target="tpu_custom_call" | custom-call | bytes 83886080 | tf_op jit(solution)/shard_map/turn/pallas_call | solution.py:1844
  397.7 0.0 reduce-scatter.6.cloned.1.call-done.down_in
  397.7 3.6 reduce-scatter.4.cloned.1.call-done.rest_ref
  401.4 0.0 reduce-scatter.8.cloned.1.call-update
  401.4 68.8 %close.1 = (f32[256,2048]{1,0:T(8,128)}, f32[64,128]{1,0:T(8,128)}, bf16[8,64,512]{2,1,0:T(8,128)(2,1)}, bf16[8,64,896]{2,1,0:T(8,128)(2,1)}) custom-call(bf16[2,1024,384]{2,1,0:T(8,128)(2,1)} %get-tuple-element.67.g_ref, bf16[2048,384]{1,0:T(8,128)(2,1)} %get-tuple-element.68.wa_ref, f32[256,2048]{1,0:T(8,128)} %get-tuple-element.69.g_mid_ref, ...), custom_call_target="tpu_custom_call" | custom-call | bytes 83886080 | tf_op jit(solution)/shard_map/close/pallas_call | solution.py:2084
  470.2 0.0 reduce-scatter.8.cloned.1.call-done.out_ref
  470.2 1.5 slice_reduce_fusion
  471.7 8.4 %exchange.1.got_ref = bf16[8,64,384]{2,1,0:T(8,128)(2,1)} custom-call(bf16[8,64,640]{2,1,0:T(8,128)(2,1)} %bitcast.6), custom_call_target="tpu_custom_call" | custom-call | bytes 13107200 | tf_op jit(solution)/shard_map/exchange/pallas_call | solution.py:342
  480.1 2.3 place_attn.1
  482.4 6.0 %place.1 = (f32[64,5632]{1,0:T(8,128)}, f32[64,5632]{1,0:T(8,128)}, f32[176,2048]{1,0:T(8,128)}, bf16[256,2048]{1,0:T(8,128)(2,1)}, f32[256,2048]{1,0:T(8,128)}) custom-call(bf16[8,64,512]{2,1,0:T(8,128)(2,1)} %get-tuple-element.76.first_in, bf16[8,64,896]{2,1,0:T(8,128)(2,1)} %get-tuple-element.77.rest_in, ...), custom_call_target="tpu_custom_call" | custom-call | tf_op jit(solution)/shard_map/place/pallas_call | solution.py:2192
  (1 shorter events, 0.0 us)
Async XLA Ops:
  7.2 390.6 %reduce-scatter.6.cloned.1.call-start = ((), (), s32[]{:S(2)}) async-start(), calls=%async_computation.4 | async-start | bytes 2293760 | tf_op jit(solution)/shard_map/reduce_scatter | solution.py:2401
  293.1 108.3 %reduce-scatter.4.cloned.1.call-start = ((), (), s32[]{:S(2)}) async-start(), calls=%async_computation.3 | async-start | bytes 4587520 | tf_op jit(solution)/shard_map/reduce_scatter | solution.py:2401
  293.8 176.3 %reduce-scatter.8.cloned.1.call-start = ((), (), s32[]{:S(2)}) async-start(), calls=%async_computation.5 | async-start | bytes 3276800 | tf_op jit(solution)/shard_map/reduce_scatter | solution.py:2401
Sparse Core Ops, SparseCore 0:
  293.2 38.1 reduce-scatter.5
  333.8 67.5 reduce-scatter.3
  403.7 52.4 reduce-scatter.7

commit v2 on v1

--- a/solution.py
+++ b/solution.py
@@ -1966,7 +1966,6 @@
             copies[-1].start()
         return mine, copies
 
-    moves = [exchange(1, rest_ref, rest_got)]
     scatter = PlaneScatter(
         lambda i: beside.at[i], lambda i: held.at[i], got, one, two, ssend, srecv
     )
@@ -1990,9 +1989,8 @@
             total = total + jnp.where(came, blocks[owner, second].astype(f32), 0.0)
         lanes_here = total.shape[1]
         first_sum[:, second * lanes_here : (second + 1) * lanes_here] = total.astype(LOW)
-    moves.append(exchange(0, first_sum, first_got))
-
     scatter.second()
+    moves = [exchange(1, rest_ref, rest_got), exchange(0, first_sum, first_got)]
 
     x = x_ref[...].astype(f32)
     inverse = norm_scale(x)

time: 500 us -> 496 us (level)
  Pallas kernels: 473 us -> 468 us
  transfers between devices with their start and end apart: 3 -> 3, of which waited for: 1 -> 1; matrix products, arithmetic and copies ran while one was open for 0% -> 0% of each run, Pallas kernels for 35% -> 34%
where the time goes in v2:
time: 496 us; the launch traced here: 491 us
  Pallas kernels  468 us (94%)
  between operations  14 us (3%)
    pallas_call x1, Pallas kernels, layer_front(): pl.pallas_call(layer_kernel, out_shape=out_shape, in_specs=[anywhere] * 1...  284 us
    pallas_call x1, Pallas kernels, layer_turn(): pl.pallas_call(turn_kernel, out_shape=[shape((rows, width), LOW), shape((...  104 us
    pallas_call x1, Pallas kernels, layer_close(): pl.pallas_call(close_kernel, out_shape=[shape((rows, width), jnp.float32)...  64.6 us
  transfers between devices with their start and end apart: 3, of which 1 were waited for; matrix products, arithmetic and copies ran while one was open for 0% of the time, Pallas kernels for 34%

profile of v2, /device:TPU:1, one launch (start us, length us, event | category | flops | bytes accessed | tf_op | source)
XLA Modules:
  0.0 490.7 jit_solution(11122825130291114482)
XLA Ops:
  7.2 0.0 reduce-scatter.6.cloned.1.call-start
  7.2 0.7 broadcast_in_dim.9
  7.9 0.7 broadcast_in_dim.10
  8.6 0.1 pad.2.clone
  8.7 0.7 maximum_maximum_fusion.gain_ref
  9.4 283.7 %layer.1 = (bf16[8,256,2048]{2,1,0:T(8,128)(2,1)}, bf16[8,256,2048]{2,1,0:T(8,128)(2,1)}, bf16[8,256,2048]{2,1,0:T(8,128)(2,1)}, bf16[8,2048,256]{2,1,0:T(8,128)...) custom-call(bf16[256,2048]{1,0:T(8,128)(2,1)} %bitcast.9, ...), custom_call_target="tpu_custom_call" | custom-call | flops 53150220288 | bytes 209715200 | tf_op jit(solution)/shard_map/layer/pallas_call | solution.py:1339
  293.1 0.0 reduce-scatter.6.cloned.1.call-update
  293.1 0.0 reduce-scatter.4.cloned.1.call-start
  293.1 0.7 reduce-scatter.4.cloned.1.call-update
  293.8 0.0 reduce-scatter.8.cloned.1.call-start
  293.9 103.8 %turn.1 = (bf16[256,2048]{1,0:T(8,128)(2,1)}, f32[256,2048]{1,0:T(8,128)}, bf16[2,1024,384]{2,1,0:T(8,128)(2,1)}, f32[8,2048]{1,0:T(8,128)}, bf16[2048,640]{1,0:T(8,128)(2,1)}) custom-call(f32[256,2048]{1,0:T(8,128)} %get-tuple-element.52.gh_ref, f32[256,2048]{1,0:T(8,128)} %get-tuple-element.53.mid_ref, bf16[256,2048]{1,0:T(8,128)(2,1)} %bitcast.8, ...), custom_call_target="tpu_custom_call" | custom-call | bytes 83886080 | tf_op jit(solution)/shard_map/turn/pallas_call | solution.py:1844
  397.7 0.0 reduce-scatter.6.cloned.1.call-done.down_in
  397.7 3.6 reduce-scatter.4.cloned.1.call-done.rest_ref
  401.4 0.0 reduce-scatter.8.cloned.1.call-update
  401.4 64.6 %close.1 = (f32[256,2048]{1,0:T(8,128)}, f32[64,128]{1,0:T(8,128)}, bf16[8,64,512]{2,1,0:T(8,128)(2,1)}, bf16[8,64,896]{2,1,0:T(8,128)(2,1)}) custom-call(bf16[2,1024,384]{2,1,0:T(8,128)(2,1)} %get-tuple-element.67.g_ref, bf16[2048,384]{1,0:T(8,128)(2,1)} %get-tuple-element.68.wa_ref, f32[256,2048]{1,0:T(8,128)} %get-tuple-element.69.g_mid_ref, ...), custom_call_target="tpu_custom_call" | custom-call | bytes 83886080 | tf_op jit(solution)/shard_map/close/pallas_call | solution.py:2082
  466.0 0.0 reduce-scatter.8.cloned.1.call-done.out_ref
  466.1 1.5 slice_reduce_fusion
  467.6 8.0 %exchange.1.got_ref = bf16[8,64,384]{2,1,0:T(8,128)(2,1)} custom-call(bf16[8,64,640]{2,1,0:T(8,128)(2,1)} %bitcast.6), custom_call_target="tpu_custom_call" | custom-call | bytes 13107200 | tf_op jit(solution)/shard_map/exchange/pallas_call | solution.py:342
  475.6 2.3 place_attn.1
  478.0 6.0 %place.1 = (f32[64,5632]{1,0:T(8,128)}, f32[64,5632]{1,0:T(8,128)}, f32[176,2048]{1,0:T(8,128)}, bf16[256,2048]{1,0:T(8,128)(2,1)}, f32[256,2048]{1,0:T(8,128)}) custom-call(bf16[8,64,512]{2,1,0:T(8,128)(2,1)} %get-tuple-element.76.first_in, bf16[8,64,896]{2,1,0:T(8,128)(2,1)} %get-tuple-element.77.rest_in, ...), custom_call_target="tpu_custom_call" | custom-call | tf_op jit(solution)/shard_map/place/pallas_call | solution.py:2190
  (1 shorter events, 0.0 us)
Async XLA Ops:
  7.2 390.6 %reduce-scatter.6.cloned.1.call-start = ((), (), s32[]{:S(2)}) async-start(), calls=%async_computation.4 | async-start | bytes 2293760 | tf_op jit(solution)/shard_map/reduce_scatter | solution.py:2399
  293.1 108.3 %reduce-scatter.4.cloned.1.call-start = ((), (), s32[]{:S(2)}) async-start(), calls=%async_computation.3 | async-start | bytes 4587520 | tf_op jit(solution)/shard_map/reduce_scatter | solution.py:2399
  293.8 172.2 %reduce-scatter.8.cloned.1.call-start = ((), (), s32[]{:S(2)}) async-start(), calls=%async_computation.5 | async-start | bytes 3276800 | tf_op jit(solution)/shard_map/reduce_scatter | solution.py:2399
Sparse Core Ops, SparseCore 0:
  293.2 38.1 reduce-scatter.5
  333.8 67.5 reduce-scatter.3
  403.7 53.5 reduce-scatter.7

commit v3 on v2

--- a/solution.py
+++ b/solution.py
@@ -1137,9 +1137,9 @@
         c.start()
     z_up[1].wait()
     z_down[1].wait()
-    lax.fori_loop(0, 4, functools.partial(forward_pass, (1,), 3, None), 0)
     z_up[2].forward()
     z_down[2].forward()
+    lax.fori_loop(0, 4, functools.partial(forward_pass, (1,), 3, None), 0)
     arrive_both(jnp.int32(4))
     for c in loads(nearest_first, 4, sources):
         c.start()

time: 496 us -> 496 us (level)
  no operation moved by 1% of the time
where the time goes in v3:
time: 496 us; the launch traced here: 490 us
  Pallas kernels  468 us (94%)
  between operations  14 us (3%)
    pallas_call x1, Pallas kernels, layer_front(): pl.pallas_call(layer_kernel, out_shape=out_shape, in_specs=[anywhere] * 1...  284 us
    pallas_call x1, Pallas kernels, layer_turn(): pl.pallas_call(turn_kernel, out_shape=[shape((rows, width), LOW), shape((...  104 us
    pallas_call x1, Pallas kernels, layer_close(): pl.pallas_call(close_kernel, out_shape=[shape((rows, width), jnp.float32)...  64.6 us
  transfers between devices with their start and end apart: 3, of which 1 were waited for; matrix products, arithmetic and copies ran while one was open for 0% of the time, Pallas kernels for 34%

profile of v3, /device:TPU:1, one launch (start us, length us, event | category | flops | bytes accessed | tf_op | source)
XLA Modules:
  0.0 490.5 jit_solution(13588908122363826170)
XLA Ops:
  7.2 0.0 reduce-scatter.6.cloned.1.call-start
  7.2 0.7 broadcast_in_dim.9
  7.9 0.7 broadcast_in_dim.10
  8.6 0.1 pad.2.clone
  8.7 0.7 maximum_maximum_fusion.gain_ref
  9.4 283.5 %layer.1 = (bf16[8,256,2048]{2,1,0:T(8,128)(2,1)}, bf16[8,256,2048]{2,1,0:T(8,128)(2,1)}, bf16[8,256,2048]{2,1,0:T(8,128)(2,1)}, bf16[8,2048,256]{2,1,0:T(8,128)...) custom-call(bf16[256,2048]{1,0:T(8,128)(2,1)} %bitcast.9, ...), custom_call_target="tpu_custom_call" | custom-call | flops 53150220288 | bytes 209715200 | tf_op jit(solution)/shard_map/layer/pallas_call | solution.py:1339
  292.9 0.0 reduce-scatter.6.cloned.1.call-update
  292.9 0.0 reduce-scatter.4.cloned.1.call-start
  293.0 0.7 reduce-scatter.4.cloned.1.call-update
  293.7 0.0 reduce-scatter.8.cloned.1.call-start
  293.7 103.8 %turn.1 = (bf16[256,2048]{1,0:T(8,128)(2,1)}, f32[256,2048]{1,0:T(8,128)}, bf16[2,1024,384]{2,1,0:T(8,128)(2,1)}, f32[8,2048]{1,0:T(8,128)}, bf16[2048,640]{1,0:T(8,128)(2,1)}) custom-call(f32[256,2048]{1,0:T(8,128)} %get-tuple-element.52.gh_ref, f32[256,2048]{1,0:T(8,128)} %get-tuple-element.53.mid_ref, bf16[256,2048]{1,0:T(8,128)(2,1)} %bitcast.8, ...), custom_call_target="tpu_custom_call" | custom-call | bytes 83886080 | tf_op jit(solution)/shard_map/turn/pallas_call | solution.py:1844
  397.5 0.0 reduce-scatter.6.cloned.1.call-done.down_in
  397.5 3.6 reduce-scatter.4.cloned.1.call-done.rest_ref
  401.1 0.0 reduce-scatter.8.cloned.1.call-update
  401.2 64.6 %close.1 = (f32[256,2048]{1,0:T(8,128)}, f32[64,128]{1,0:T(8,128)}, bf16[8,64,512]{2,1,0:T(8,128)(2,1)}, bf16[8,64,896]{2,1,0:T(8,128)(2,1)}) custom-call(bf16[2,1024,384]{2,1,0:T(8,128)(2,1)} %get-tuple-element.67.g_ref, bf16[2048,384]{1,0:T(8,128)(2,1)} %get-tuple-element.68.wa_ref, f32[256,2048]{1,0:T(8,128)} %get-tuple-element.69.g_mid_ref, ...), custom_call_target="tpu_custom_call" | custom-call | bytes 83886080 | tf_op jit(solution)/shard_map/close/pallas_call | solution.py:2082
  465.8 0.0 reduce-scatter.8.cloned.1.call-done.out_ref
  465.8 1.5 slice_reduce_fusion
  467.4 8.0 %exchange.1.got_ref = bf16[8,64,384]{2,1,0:T(8,128)(2,1)} custom-call(bf16[8,64,640]{2,1,0:T(8,128)(2,1)} %bitcast.6), custom_call_target="tpu_custom_call" | custom-call | bytes 13107200 | tf_op jit(solution)/shard_map/exchange/pallas_call | solution.py:342
  475.4 2.3 place_attn.1
  477.7 6.0 %place.1 = (f32[64,5632]{1,0:T(8,128)}, f32[64,5632]{1,0:T(8,128)}, f32[176,2048]{1,0:T(8,128)}, bf16[256,2048]{1,0:T(8,128)(2,1)}, f32[256,2048]{1,0:T(8,128)}) custom-call(bf16[8,64,512]{2,1,0:T(8,128)(2,1)} %get-tuple-element.76.first_in, bf16[8,64,896]{2,1,0:T(8,128)(2,1)} %get-tuple-element.77.rest_in, ...), custom_call_target="tpu_custom_call" | custom-call | tf_op jit(solution)/shard_map/place/pallas_call | solution.py:2190
  (1 shorter events, 0.0 us)
Async XLA Ops:
  7.2 390.4 %reduce-scatter.6.cloned.1.call-start = ((), (), s32[]{:S(2)}) async-start(), calls=%async_computation.4 | async-start | bytes 2293760 | tf_op jit(solution)/shard_map/reduce_scatter | solution.py:2399
  292.9 108.2 %reduce-scatter.4.cloned.1.call-start = ((), (), s32[]{:S(2)}) async-start(), calls=%async_computation.3 | async-start | bytes 4587520 | tf_op jit(solution)/shard_map/reduce_scatter | solution.py:2399
  293.7 172.2 %reduce-scatter.8.cloned.1.call-start = ((), (), s32[]{:S(2)}) async-start(), calls=%async_computation.5 | async-start | bytes 3276800 | tf_op jit(solution)/shard_map/reduce_scatter | solution.py:2399
Sparse Core Ops, SparseCore 0:
  293.0 38.2 reduce-scatter.5
  333.6 67.5 reduce-scatter.3
  403.4 53.5 reduce-scatter.7
